TPU v7x, 32 devices: a whole 2x2x4 slice. The times are simulated.
32 devices in a mesh: dp: 8 (over z, core), mp: 4 (over y, x).
Axes of the slice: x: 2, y: 2, z: 4, core: 2. Of those that a mesh axis runs over, the one named last changes fastest.
Arguments:
- inputs: bfloat16 [8, 48, 48, 3072], P('dp', 'mp'), may hold values from -6 to 6
- cotangent: bfloat16 [8, 48, 48, 3072], P('dp', 'mp'), may hold values from -6 to 6
- mode_weights: bfloat16 [2, 256, 7, 4096], P(None, 'mp'), may hold values from -4.1875 to 4.1875
- local_weight: bfloat16 [64, 64], replicated, may hold values from -0.75 to 0.75
- local_bias: float32 [64], replicated, may hold values from -3 to 3
Outputs:
- outputs: bfloat16 [8, 48, 48, 3072], P('dp', 'mp')
- input_grads: bfloat16 [8, 48, 48, 3072], P('dp', 'mp')
- mode_grads: float32 [2, 256, 7, 4096], P(None, 'mp')
All inputs are finite; a program needn't handle non-finite values.
Results may differ from a plain program's by a relative error of at most 0.0012.
Values sent between devices are 32-bit elements; how exact they have to be, the bound alone decides.
A program may use at most 192 MiB of HBM per device.

v0:
```python
import functools
import math

import jax
import jax.numpy as jnp
from jax import lax
from jax.sharding import PartitionSpec as P

MX = 8


highest = lax.Precision.HIGHEST


def kept_freqs(count, length):
    lowest = lax.iota(jnp.int32, count)
    return jnp.concatenate([lowest, length - count + lowest])


def angle_tables(freqs, length):
    places = lax.iota(jnp.int32, length)
    turns = freqs[:, None] * places[None, :] % length
    angles = turns.astype(jnp.float32) * (2.0 * math.pi / length)
    return (jnp.cos(angles), jnp.sin(angles))


def forward_xy(field, cos_xy, sin_xy, chan):
    first_real = jnp.einsum("ax,szxw->szaw", cos_xy, field, precision=highest)
    first_imag = -jnp.einsum("ax,szxw->szaw", sin_xy, field, precision=highest)
    samples, planes, count, row_width = first_real.shape
    shaped = (samples, planes, count, row_width // chan, chan)
    first_real = first_real.reshape(shaped)
    first_imag = first_imag.reshape(shaped)
    second_real = jnp.einsum("by,szayc->szabc", cos_xy, first_real, precision=highest) + jnp.einsum(
        "by,szayc->szabc", sin_xy, first_imag, precision=highest
    )
    second_imag = jnp.einsum("by,szayc->szabc", cos_xy, first_imag, precision=highest) - jnp.einsum(
        "by,szayc->szabc", sin_xy, first_real, precision=highest
    )
    packed = jnp.concatenate([second_real, second_imag], axis=4)
    return packed.reshape(samples, planes, count * count, 2 * chan)


def inverse_xy(packed, cos_xy, sin_xy, chan, grid):
    samples, planes, pair_count, doubled = packed.shape
    count = cos_xy.shape[0]
    blocks = packed.reshape(samples, planes, count, count, doubled)
    block_real = blocks[..., :chan]
    block_imag = blocks[..., chan:]
    middle_real = jnp.einsum("by,szabc->szayc", cos_xy, block_real, precision=highest) - jnp.einsum(
        "by,szabc->szayc", sin_xy, block_imag, precision=highest
    )
    middle_imag = jnp.einsum("by,szabc->szayc", cos_xy, block_imag, precision=highest) + jnp.einsum(
        "by,szabc->szayc", sin_xy, block_real, precision=highest
    )
    field = jnp.einsum("ax,szayc->szxyc", cos_xy, middle_real, precision=highest) - jnp.einsum(
        "ax,szayc->szxyc", sin_xy, middle_imag, precision=highest
    )
    return field.reshape(samples, planes, grid, grid * chan)


def z_forward(piece, cos_z, sin_z, chan):
    part_real = piece[..., :chan]
    part_imag = piece[..., chan:]
    mode_real = jnp.einsum("kz,szpc->spkc", cos_z, part_real, precision=highest) + jnp.einsum(
        "kz,szpc->spkc", sin_z, part_imag, precision=highest
    )
    mode_imag = jnp.einsum("kz,szpc->spkc", cos_z, part_imag, precision=highest) - jnp.einsum(
        "kz,szpc->spkc", sin_z, part_real, precision=highest
    )
    return (mode_real, mode_imag)


def z_inverse(mode_real, mode_imag, cos_z, sin_z):
    line_real = jnp.einsum("kz,spkc->szpc", cos_z, mode_real, precision=highest) - jnp.einsum(
        "kz,spkc->szpc", sin_z, mode_imag, precision=highest
    )
    line_imag = jnp.einsum("kz,spkc->szpc", cos_z, mode_imag, precision=highest) + jnp.einsum(
        "kz,spkc->szpc", sin_z, mode_real, precision=highest
    )
    return jnp.concatenate([line_real, line_imag], axis=3)


def mode_terms(values, cotans, chan):
    value_real = values[..., :chan]
    value_imag = values[..., chan:]
    cotan_real = cotans[..., :chan]
    cotan_imag = cotans[..., chan:]
    term_real = jnp.einsum(
        "spki,spko->pkio", value_real, cotan_real, precision=highest
    ) + jnp.einsum("spki,spko->pkio", value_imag, cotan_imag, precision=highest)
    term_imag = jnp.einsum(
        "spki,spko->pkio", value_real, cotan_imag, precision=highest
    ) - jnp.einsum("spki,spko->pkio", value_imag, cotan_real, precision=highest)
    return jnp.stack([term_real, term_imag])


def on_device(inputs, cotangent, mode_weights, local_weight, local_bias):
    grid = inputs.shape[2]
    chan = local_weight.shape[0]
    pairs_here = mode_weights.shape[1]
    zmodes = mode_weights.shape[2]
    cos_xy, sin_xy = angle_tables(kept_freqs(MX, grid), grid)
    zfreqs = lax.iota(jnp.int32, zmodes)
    cos_z, sin_z = angle_tables(zfreqs, grid)
    z_scale = jnp.where(zfreqs == 0, 1.0, 2.0).astype(jnp.float32) / float(grid * grid * grid)
    z_scale = z_scale[None, None, :, None]
    weights = mode_weights.astype(jnp.float32).reshape(2, pairs_here, zmodes, chan, chan)
    weight_real = weights[0]
    weight_imag = weights[1]
    field = inputs.astype(jnp.float32)
    plane_spectra = forward_xy(field, cos_xy, sin_xy, chan)
    mode_real, mode_imag = z_forward(
        lax.all_to_all(plane_spectra, "mp", split_axis=2, concat_axis=1, tiled=True),
        cos_z,
        sin_z,
        chan,
    )
    mixed_real = jnp.einsum(
        "spki,pkio->spko", mode_real, weight_real, precision=highest
    ) - jnp.einsum("spki,pkio->spko", mode_imag, weight_imag, precision=highest)
    mixed_imag = jnp.einsum(
        "spki,pkio->spko", mode_real, weight_imag, precision=highest
    ) + jnp.einsum("spki,pkio->spko", mode_imag, weight_real, precision=highest)
    lines = z_inverse(mixed_real * z_scale, mixed_imag * z_scale, cos_z, sin_z)
    returned = lax.all_to_all(lines, "mp", split_axis=1, concat_axis=2, tiled=True)
    returned, spectra = (returned, jnp.concatenate([mode_real, mode_imag], axis=3))
    spectral = inverse_xy(returned, cos_xy, sin_xy, chan, grid)
    local = jnp.dot(inputs.reshape(-1, chan), local_weight, preferred_element_type=jnp.float32)
    pre = spectral + local.reshape(spectral.shape) + jnp.tile(local_bias, grid)
    gelu_fn = functools.partial(jax.nn.gelu, approximate=True)
    active, gelu_pull = jax.vjp(gelu_fn, pre)
    (slope,) = gelu_pull(cotangent.astype(jnp.float32))
    outputs = active.astype(jnp.bfloat16)
    slope_spectra = forward_xy(slope, cos_xy, sin_xy, chan)
    cot_real, cot_imag = z_forward(
        lax.all_to_all(slope_spectra, "mp", split_axis=2, concat_axis=1, tiled=True),
        cos_z,
        sin_z,
        chan,
    )
    cot_real = cot_real * z_scale
    cot_imag = cot_imag * z_scale
    back_real = jnp.einsum(
        "spko,pkio->spki", cot_real, weight_real, precision=highest
    ) + jnp.einsum("spko,pkio->spki", cot_imag, weight_imag, precision=highest)
    back_imag = jnp.einsum(
        "spko,pkio->spki", cot_imag, weight_real, precision=highest
    ) - jnp.einsum("spko,pkio->spki", cot_real, weight_imag, precision=highest)
    lines = z_inverse(back_real, back_imag, cos_z, sin_z)
    returned = lax.all_to_all(lines, "mp", split_axis=1, concat_axis=2, tiled=True)
    cot_spectra = jnp.concatenate([cot_real, cot_imag], axis=3)
    spectral_grad = inverse_xy(returned, cos_xy, sin_xy, chan, grid)
    local_grad = jnp.dot(
        slope.reshape(-1, chan), local_weight.astype(jnp.float32).T, precision=highest
    )
    input_grads = (spectral_grad + local_grad.reshape(spectral_grad.shape)).astype(jnp.bfloat16)
    summed = lax.psum(mode_terms(spectra, cot_spectra, chan), "dp")
    mode_grads = summed.reshape(2, pairs_here, zmodes, chan * chan)
    return (outputs, input_grads, mode_grads)


def solution(mesh):
    placed = (
        P("dp", "mp", None, None),
        P("dp", "mp", None, None),
        P(None, "mp", None, None),
        P(),
        P(),
    )
    return jax.shard_map(
        on_device,
        mesh=mesh,
        in_specs=placed,
        out_specs=(P("dp", "mp", None, None), P("dp", "mp", None, None), P(None, "mp", None, None)),
        check_vma=False,
    )
```

profile of v0, /device:TPU:0, one launch (start us, length us, event | category | flops | bytes accessed | tf_op | source)
XLA Modules:
  0.0 718.2 jit_solution(1292959680495252092)
XLA Ops:
  7.3 5.2 fusion.44
  12.5 3.0 convolution_bitcast_fusion
  15.5 5.2 reshape.395
  20.7 6.1 fusion.107
  26.8 4.8 reshape.394
  31.6 4.7 fusion.109
  36.4 4.6 subtract_bitcast_fusion.8
  41.0 2.6 add_bitcast_fusion.6
  44.2 2.8 copy.88
  46.9 15.7 %all-to-all-start = ((f32[1,12,256,128]{3,0,1,2:T(1,128)}), f32[1,12,256,128]{3,0,1,2:T(1,128)}, u32[]{:S(2)}, u32[]{:S(2)}) async-start(f32[1,12,256,128]{3,0,1,2:T(1,128)} %copy.88), calls=%async_computation | async-start | bytes 3145728 | tf_op jit(solution)/shard_map/all_to_all | solution.py:114
  62.6 6.9 reshape.407
  70.9 7.2 %fusion.448 = (bf16[1,64,7,4096]{3,1,2,0:T(8,128)(2,1)}, bf16[1,64,7,4096]{3,1,2,0:T(8,128)(2,1)}) fusion(bf16[2,64,7,4096]{3,1,2,0:T(8,128)(2,1)} %param.7), kind=kLoop, calls=%fused_computation.407 | loop fusion | bytes 14680064 | tf_op jit(solution)/shard_map/slice | solution.py:110
  78.1 11.0 %squeeze.7 = bf16[64,7,64,64]{3,2,0,1:T(8,128)(2,1)} reshape(bf16[1,64,7,4096]{3,1,2,0:T(8,128)(2,1)} %get-tuple-element.5) | data formatting | bytes 7340032 | tf_op jit(solution)/shard_map/squeeze | solution.py:110
  89.2 11.1 %squeeze.6 = bf16[64,7,64,64]{3,2,0,1:T(8,128)(2,1)} reshape(bf16[1,64,7,4096]{3,1,2,0:T(8,128)(2,1)} %get-tuple-element.6) | data formatting | bytes 7340032 | tf_op jit(solution)/shard_map/squeeze | solution.py:109
  109.8 6.3 fusion.17
  116.1 5.9 fusion.19
  121.9 6.0 fusion.25
  128.0 5.9 fusion.27
  142.0 4.7 all-to-all-start.1
  146.7 10.3 %fusion.451 = f32[27648,64]{1,0:T(8,128)} fusion(bf16[27648,64]{1,0:T(8,128)(2,1)} %reshape.407, bf16[64,64]{1,0:T(8,128)(2,1)S(1)} %copy-done), kind=kOutput, calls=%fused_computation.410 | convolution fusion | flops 226492416 | bytes 10625024 | tf_op jit(solution)/shard_map/dot_general | solution.py:129
  156.9 12.9 %reshape.408 = f32[1,12,48,3072]{3,2,1,0:T(8,128)} reshape(f32[27648,64]{1,0:T(8,128)} %fusion.451) | data formatting | bytes 14155776 | tf_op jit(solution)/shard_map/reshape | solution.py:130
  170.0 4.1 fusion.56
  174.1 4.1 fusion.55
  178.2 4.1 add_bitcast_fusion.2
  182.3 4.3 subtract_bitcast_fusion.4
  186.6 12.3 %fusion.33 = f32[12,48,64,48]{2,3,1,0:T(8,128)S(1)} fusion(f32[12,16,48,64]{3,2,1,0:T(8,128)S(1)} %subtract_bitcast_fusion.4, s32[16]{0:T(128)S(1)} %copy-done.12), kind=kOutput, calls=%fused_computation.45 | convolution fusion | flops 339745536 | bytes 9437248 | tf_op jit(solution)/shard_map/ax,szayc->szxyc/dot_general | solution.py:56
  198.9 15.2 %subtract_bitcast_fusion.2 = f32[1,12,48,48,64]{4,2,3,1,0:T(8,128)} fusion(f32[12,48,64,48]{2,3,1,0:T(8,128)S(1)} %fusion.33, f32[12,16,48,64]{3,2,1,0:T(8,128)S(1)} %add_bitcast_fusion.2, s32[16]{0:T(128)S(1)} %copy-done.12), kind=kOutput, calls=%fused_computation.4 | convolution fusion | flops 341515008 | bytes 16515136 | tf_op jit(solution)/shard_map/ax,szayc->szxyc/dot_general | solution.py:56
  214.1 14.3 %copy.97 = f32[1,12,48,48,64]{4,3,2,1,0:T(8,128)} copy(f32[1,12,48,48,64]{4,2,3,1,0:T(8,128)} %subtract_bitcast_fusion.2) | data formatting | bytes 14155776 | tf_op jit(solution)/shard_map/sub | solution.py:56
  228.4 12.7 %reshape.406 = f32[1,12,48,3072]{3,2,1,0:T(8,128)} reshape(f32[1,12,48,48,64]{4,3,2,1,0:T(8,128)} %copy.97) | data formatting | bytes 14155776 | tf_op jit(solution)/shard_map/reshape | solution.py:59
  241.1 10.3 %fusion.1 = (f32[1,12,48,3072]{3,2,1,0:T(8,128)S(1)}, bf16[1,12,48,3072]{3,2,1,0:T(8,128)(2,1)}) fusion(bf16[1,12,48,3072]{3,2,1,0:T(8,128)(2,1)S(1)} %copy-done.5, f32[3072]{0:T(1024)} %add.256, f32[1,12,48,3072]{3,2,1,0:T(8,128)} %reshape.406, f32[1,12,48,3072]{3,2,1,0:T(8,128)} %reshape.408), kind=kLoop, calls=%fused_computation.10 | loop fusion | flops 42467328 | bytes 28323840 | tf_op jit(solution)/shard_map/transpose(jvp())/add_any | solution.py:132
  251.4 5.3 fusion.41
  256.7 4.0 fusion.35
  260.6 4.8 reshape.411
  265.5 6.1 fusion.100
  271.6 3.2 reshape.410
  274.8 4.9 fusion.102
  279.7 4.6 subtract_bitcast_fusion.6
  284.4 2.6 add_bitcast_fusion.4
  287.5 2.8 copy.99
  290.3 4.2 all-to-all-start.2
  296.0 11.8 %reshape.423 = f32[27648,64]{1,0:T(8,128)} reshape(f32[1,12,48,3072]{3,2,1,0:T(8,128)} %copy-done.1) | data formatting | bytes 14155776 | tf_op jit(solution)/shard_map/reshape | solution.py:155
  307.8 5.4 all-to-all-done.2
  319.5 13.9 %fusion.13 = f32[64,7,1,64]{3,2,1,0:T(1,128)S(1)} fusion(bf16[64,7,64,64]{3,2,0,1:T(8,128)(2,1)} %squeeze.7, f32[64,7,64,1]{2,1,0,3:T(8,128)S(1)} %bitcast.399), kind=kOutput, calls=%fused_computation.25 | convolution fusion | flops 22020096 | bytes 3899392 | tf_op jit(solution)/shard_map/spko,pkio->spki/dot_general | solution.py:149
  333.4 11.4 %fusion.23 = f32[64,7,1,64]{3,2,1,0:T(1,128)S(1)} fusion(bf16[64,7,64,64]{3,2,0,1:T(8,128)(2,1)S(1)} %bitcast.385, f32[64,7,64,1]{2,1,0,3:T(8,128)S(1)} %bitcast.400), kind=kOutput, calls=%fused_computation.35 | convolution fusion | flops 22020096 | bytes 3899392 | tf_op jit(solution)/shard_map/spko,pkio->spki/dot_general | solution.py:144
  344.9 1.8 fusion.66
  346.7 11.6 %fusion.15 = f32[64,7,1,64]{3,2,1,0:T(1,128)S(1)} fusion(bf16[64,7,64,64]{3,2,0,1:T(8,128)(2,1)S(1)} %bitcast.389, f32[64,7,64,1]{2,1,0,3:T(8,128)S(1)} %bitcast.396), kind=kOutput, calls=%fused_computation.27 | convolution fusion | flops 22020096 | bytes 3899392 | tf_op jit(solution)/shard_map/spko,pkio->spki/dot_general | solution.py:146
  359.8 8.8 %add_bitcast_fusion = (f32[1,64,7,64,64]{4,3,1,2,0:T(8,128)S(1)}, f32[1,64,7,64,64]{4,3,1,2,0:T(8,128)S(1)}) fusion(f32[64,7,64]{2,0,1:T(8,128)} %copy.113, f32[64,7,64]{2,0,1:T(8,128)} %copy.112, f32[64,7,64]{2,0,1:T(8,128)} %copy.111, f32[64,7,64]{2,0,1:T(8,128)} %copy.110), kind=kLoop, calls=%fused_computation.2 | loop fusion | flops 11010048 | bytes 15138816 | tf_op jit(solution)/shard_map/stack | solution.py:95
  368.7 10.6 %pad_maximum_fusion = f32[2,64,7,64,64]{4,3,1,2,0:T(8,128)} fusion(f32[1,64,7,64,64]{4,3,1,2,0:T(8,128)S(1)} %get-tuple-element.12, f32[1,64,7,64,64]{4,3,1,2,0:T(8,128)S(1)} %get-tuple-element.11), kind=kLoop, calls=%fused_computation | loop fusion | flops 3670016 | bytes 29360128 | tf_op jit(solution)/shard_map/stack | solution.py:95
  379.3 24.7 %reshape.425 = f32[2,64,7,4096]{3,1,2,0:T(8,128)} reshape(f32[2,64,7,64,64]{4,3,1,2,0:T(8,128)} %pad_maximum_fusion) | data formatting | bytes 29360128 | tf_op jit(solution)/shard_map/reshape | solution.py:159
  404.0 14.0 %fusion.21 = f32[64,7,1,64]{3,2,1,0:T(1,128)S(1)} fusion(bf16[64,7,64,64]{3,2,0,1:T(8,128)(2,1)} %squeeze.6, f32[64,7,64,1]{2,1,0,3:T(8,128)S(1)} %bitcast.398), kind=kOutput, calls=%fused_computation.33 | convolution fusion | flops 22020096 | bytes 3899392 | tf_op jit(solution)/shard_map/spko,pkio->spki/dot_general | solution.py:147
  426.2 3.6 all-to-all-start.3
  429.8 12.9 %fusion.452 = f32[27648,64]{1,0:T(8,128)} fusion(f32[27648,64]{1,0:T(8,128)} %reshape.423, bf16[64,64]{1,0:T(8,128)(2,1)S(1)} %copy-done), kind=kOutput, calls=%fused_computation.411 | convolution fusion | flops 1358954496 | bytes 14163968 | tf_op jit(solution)/shard_map/dot_general | solution.py:154
  442.7 12.7 %reshape.424 = f32[1,12,48,3072]{3,2,1,0:T(8,128)} reshape(f32[27648,64]{1,0:T(8,128)} %fusion.452) | data formatting | bytes 14155776 | tf_op jit(solution)/shard_map/reshape | solution.py:157
  455.5 4.1 fusion.58
  459.6 4.1 fusion.57
  463.7 4.1 add_bitcast_fusion.1
  467.8 4.3 subtract_bitcast_fusion.3
  472.2 12.4 %fusion.30 = f32[12,48,64,48]{2,3,1,0:T(8,128)S(1)} fusion(f32[12,16,48,64]{3,2,1,0:T(8,128)S(1)} %subtract_bitcast_fusion.3, s32[16]{0:T(128)S(1)} %copy-done.14), kind=kOutput, calls=%fused_computation.42 | convolution fusion | flops 339745536 | bytes 9437248 | tf_op jit(solution)/shard_map/ax,szayc->szxyc/dot_general | solution.py:56
  484.6 14.9 %subtract_bitcast_fusion.1 = f32[1,12,48,48,64]{4,2,3,1,0:T(8,128)} fusion(f32[12,48,64,48]{2,3,1,0:T(8,128)S(1)} %fusion.30, f32[12,16,48,64]{3,2,1,0:T(8,128)S(1)} %add_bitcast_fusion.1, s32[16]{0:T(128)S(1)} %copy-done.14), kind=kOutput, calls=%fused_computation.3 | convolution fusion | flops 341515008 | bytes 16515136 | tf_op jit(solution)/shard_map/ax,szayc->szxyc/dot_general | solution.py:56
  499.5 14.3 %copy.108 = f32[1,12,48,48,64]{4,3,2,1,0:T(8,128)} copy(f32[1,12,48,48,64]{4,2,3,1,0:T(8,128)} %subtract_bitcast_fusion.1) | data formatting | bytes 14155776 | tf_op jit(solution)/shard_map/sub | solution.py:56
  513.9 12.6 %reshape.422 = f32[1,12,48,3072]{3,2,1,0:T(8,128)} reshape(f32[1,12,48,48,64]{4,3,2,1,0:T(8,128)} %copy.108) | data formatting | bytes 14155776 | tf_op jit(solution)/shard_map/reshape | solution.py:59
  526.5 8.1 %add_convert_fusion = bf16[1,12,48,3072]{3,2,1,0:T(8,128)(2,1)} fusion(f32[1,12,48,3072]{3,2,1,0:T(8,128)} %reshape.422, f32[1,12,48,3072]{3,2,1,0:T(8,128)} %reshape.424), kind=kLoop, calls=%fused_computation.22 | loop fusion | flops 3538944 | bytes 17694720 | tf_op jit(solution)/shard_map/convert_element_type | solution.py:157
  534.6 164.1 %all-reduce.2.cloned.1.call-done = f32[2,64,7,4096]{3,1,2,0:T(8,128)} async-done(((f32[2,64,7,4096]{3,1,2,0:T(8,128)}), f32[2,64,7,4096]{3,1,2,0:T(8,128)}) %all-reduce.2.cloned.1.call-update) | async-done | bytes 14680080 | tf_op jit(solution)/shard_map/psum | solution.py:158
  698.7 12.5 %copy.229 = f32[2,64,7,4096]{3,1,2,0:T(8,128)} copy(f32[2,64,7,4096]{3,1,2,0:T(8,128)} %all-reduce.2.cloned.1.call-done) | data formatting | bytes 29360128
  (108 shorter events, 37.6 us)
Async XLA Ops:
  7.2 139.5 %copy-start = (bf16[64,64]{1,0:T(8,128)(2,1)S(1)}, bf16[64,64]{1,0:T(8,128)(2,1)}, u32[]{:S(2)}) copy-start(bf16[64,64]{1,0:T(8,128)(2,1)} %param.8) | copy-start | bytes 24580
  7.2 5.3 copy-start.2
  7.3 5.2 copy-start.10
  31.6 4.7 copy-start.3
  31.6 4.7 copy-start.11
  31.6 9.4 %slice-start = ((s8[4718592]{0:T(1024)(128)(4,1)}), s8[4194304]{0:T(1024)(128)(4,1)S(1)}, s32[]{:S(2)}) async-start(s8[4718592]{0:T(1024)(128)(4,1)} %bitcast.368), calls=%async_computation.5 | async-start | bytes 8388608
  36.4 4.7 slice-start.1
  46.9 53.3 %all-to-all-start = ((f32[1,12,256,128]{3,0,1,2:T(1,128)}), f32[1,12,256,128]{3,0,1,2:T(1,128)}, u32[]{:S(2)}, u32[]{:S(2)}) async-start(f32[1,12,256,128]{3,0,1,2:T(1,128)} %copy.88), calls=%async_computation | async-start | bytes 3145728 | tf_op jit(solution)/shard_map/all_to_all | solution.py:114
  100.2 38.1 %copy-start.15 = (f32[7]{0:T(128)}, f32[7]{0:T(128)S(1)}, u32[]{:S(2)}) copy-start(f32[7]{0:T(128)S(1)} %fusion.327) | copy-start | bytes 88
  101.9 7.9 %slice-start.8 = ((s8[7340032]{0:T(1024)(128)(4,1)}), s8[4194304]{0:T(1024)(128)(4,1)S(1)}, s32[]{:S(2)}) async-start(s8[7340032]{0:T(1024)(128)(4,1)} %bitcast.386), calls=%async_computation.13 | async-start | bytes 8388608
  102.5 7.3 %slice-start.9 = ((s8[7340032]{0:T(1024)(128)(4,1)}), s8[3145728]{0:T(1024)(128)(4,1)S(1)}, s32[]{:S(2)}) async-start(s8[7340032]{0:T(1024)(128)(4,1)} %bitcast.386), calls=%async_computation.14 | async-start | bytes 6291456
  107.9 20.0 %copy-start.6 = (f32[64,64,7]{1,2,0:T(8,128)}, f32[64,64,7]{1,2,0:T(8,128)S(1)}, u32[]{:S(2)}) copy-start(f32[64,64,7]{1,2,0:T(8,128)S(1)} %fusion.61) | copy-start | bytes 344068
  109.8 12.2 %copy-start.8 = (f32[64,64,7]{1,2,0:T(8,128)}, f32[64,64,7]{1,2,0:T(8,128)S(1)}, u32[]{:S(2)}) copy-start(f32[64,64,7]{1,2,0:T(8,128)S(1)} %fusion.62) | copy-start | bytes 344068
  109.8 12.1 %slice-start.4 = ((s8[7340032]{0:T(1024)(128)(4,1)}), s8[4194304]{0:T(1024)(128)(4,1)S(1)}, s32[]{:S(2)}) async-start(s8[7340032]{0:T(1024)(128)(4,1)} %bitcast.382), calls=%async_computation.9 | async-start | bytes 8388608
  116.1 5.9 slice-start.5
  142.0 27.9 %all-to-all-start.1 = ((f32[1,48,64,128]{3,2,0,1:T(8,128)}), f32[1,48,64,128]{3,2,0,1:T(8,128)S(1)}, u32[]{:S(2)}, u32[]{:S(2)}) async-start(f32[1,48,64,128]{3,2,0,1:T(8,128)} %copy.93), calls=%async_computation.1 | async-start | bytes 3145728 | tf_op jit(solution)/shard_map/all_to_all | solution.py:126
  156.9 13.1 %copy-start.12 = (s32[16]{0:T(128)S(1)}, s32[16]{0:T(128)}, u32[]{:S(2)}) copy-start(s32[16]{0:T(128)} %copy-done.10) | copy-start | bytes 196
  228.4 12.7 %copy-start.5 = (bf16[1,12,48,3072]{3,2,1,0:T(8,128)(2,1)S(1)}, bf16[1,12,48,3072]{3,2,1,0:T(8,128)(2,1)}, u32[]{:S(2)}) copy-start(bf16[1,12,48,3072]{3,2,1,0:T(8,128)(2,1)} %param.6) | copy-start | bytes 10616836
  241.1 10.3 %copy-start.13 = (s32[16]{0:T(128)S(1)}, s32[16]{0:T(128)}, u32[]{:S(2)}) copy-start(s32[16]{0:T(128)} %copy-done.10) | copy-start | bytes 196
  251.3 5.3 copy-start.1
  260.6 4.8 copy-start.14
  274.8 4.9 copy-start.4
  274.8 9.6 %slice-start.2 = ((s8[4718592]{0:T(1024)(128)(4,1)}), s8[4194304]{0:T(1024)(128)(4,1)S(1)}, s32[]{:S(2)}) async-start(s8[4718592]{0:T(1024)(128)(4,1)} %bitcast.370), calls=%async_computation.7 | async-start | bytes 8388608
  279.7 4.7 slice-start.3
  287.0 7.5 %copy-start.7 = (f32[64,64,7]{1,2,0:T(8,128)S(1)}, f32[64,64,7]{1,2,0:T(8,128)}, u32[]{:S(2)}) copy-start(f32[64,64,7]{1,2,0:T(8,128)} %copy-done.6) | copy-start | bytes 344068
  287.0 8.2 %copy-start.9 = (f32[64,64,7]{1,2,0:T(8,128)S(1)}, f32[64,64,7]{1,2,0:T(8,128)}, u32[]{:S(2)}) copy-start(f32[64,64,7]{1,2,0:T(8,128)} %copy-done.8) | copy-start | bytes 344068
  290.3 22.9 %all-to-all-start.2 = ((f32[1,12,256,128]{3,0,1,2:T(1,128)}), f32[1,12,256,128]{3,0,1,2:T(1,128)S(1)}, u32[]{:S(2)}, u32[]{:S(2)}) async-start(f32[1,12,256,128]{3,0,1,2:T(1,128)} %copy.99), calls=%async_computation.2 | async-start | bytes 3145728 | tf_op jit(solution)/shard_map/all_to_all | solution.py:137
  294.5 404.2 %all-reduce.2.cloned.1.call-start = ((), (), s32[]{:S(2)}) async-start(), calls=%async_computation.4 | async-start | bytes 29360128 | tf_op jit(solution)/shard_map/psum | solution.py:158
  313.4 4.3 copy-start.16
  313.4 20.0 %slice-start.6 = ((s8[7340032]{0:T(1024)(128)(4,1)}), s8[4194304]{0:T(1024)(128)(4,1)S(1)}, s32[]{:S(2)}) async-start(s8[7340032]{0:T(1024)(128)(4,1)} %bitcast.384), calls=%async_computation.11 | async-start | bytes 8388608
  315.8 17.6 %slice-start.7 = ((s8[7340032]{0:T(1024)(128)(4,1)}), s8[3145728]{0:T(1024)(128)(4,1)S(1)}, s32[]{:S(2)}) async-start(s8[7340032]{0:T(1024)(128)(4,1)} %bitcast.384), calls=%async_computation.12 | async-start | bytes 6291456
  319.5 27.2 %slice-start.10 = ((s8[7340032]{0:T(1024)(128)(4,1)}), s8[4194304]{0:T(1024)(128)(4,1)S(1)}, s32[]{:S(2)}) async-start(s8[7340032]{0:T(1024)(128)(4,1)} %bitcast.388), calls=%async_computation.15 | async-start | bytes 8388608
  333.4 13.3 %slice-start.11 = ((s8[7340032]{0:T(1024)(128)(4,1)}), s8[3145728]{0:T(1024)(128)(4,1)S(1)}, s32[]{:S(2)}) async-start(s8[7340032]{0:T(1024)(128)(4,1)} %bitcast.388), calls=%async_computation.16 | async-start | bytes 6291456
  426.2 29.2 %all-to-all-start.3 = ((f32[1,48,64,128]{3,2,0,1:T(8,128)}), f32[1,48,64,128]{3,2,0,1:T(8,128)S(1)}, u32[]{:S(2)}, u32[]{:S(2)}) async-start(f32[1,48,64,128]{3,2,0,1:T(8,128)} %copy.104), calls=%async_computation.3 | async-start | bytes 3145728 | tf_op jit(solution)/shard_map/all_to_all | solution.py:151
Sparse Core Ops, SparseCore 0:
  404.2 294.4 all-reduce.1
where the time goes:
time: 718 us
  matrix products  266 us (37%)
  local copies, waits for them, and re-layouts  199 us (28%)
  waiting for transfers between devices  169 us (24%)
  other arithmetic  39.8 us (6%)
  starting transfers between devices  28.1 us (4%)
  between operations  15 us (2%)
    psum x1, waiting for transfers between devices, on_device(): summed = lax.psum(mode_terms(spectra, cot_spectra, chan), 'dp')  164 us
    dot_general x2, matrix products, inverse_xy(): jnp.einsum('ax,szayc->szxyc', sin_xy, middle_imag, precision=highest)  30.1 us
    sub x2, local copies, waits for them, and re-layouts, inverse_xy(): jnp.einsum('ax,szayc->szxyc', cos_xy, middle_real, precision=highest)  28.7 us
    reshape x2, local copies, waits for them, and re-layouts, inverse_xy(): return field.reshape(samples, planes, grid, grid * chan)  25.3 us
    reshape x1, local copies, waits for them, and re-layouts, on_device(): mode_grads = summed.reshape(2, pairs_here, zmodes, chan * chan)  24.7 us
    dot_general x2, matrix products, inverse_xy(): jnp.einsum('ax,szayc->szxyc', cos_xy, middle_real, precision=highest)  24.7 us
    another operation x8, local copies, waits for them, and re-layouts  21 us
    another operation x2, other arithmetic, mode_terms(): return jnp.stack([term_real, term_imag])  19.4 us
  transfers between devices with their start and end apart: 5, of which 2 were waited for; matrix products, arithmetic and copies ran while one was open for 28% of the time, Pallas kernels for 0%

commit v1 on v0

v1 whole, which is shorter than its diff:
```python
import functools
import math

import jax
import jax.numpy as jnp
import ml_dtypes
import numpy as np
from jax import lax
from jax.experimental import pallas as pl
from jax.experimental.pallas import tpu as pltpu
from jax.sharding import PartitionSpec as P

MX = 8
LANES = 128
WIDE = 256
ROWS = 8
F32 = jnp.float32
BF16 = jnp.bfloat16
PARAMS = dict(vmem_limit_bytes=50 * 2**20)


def mm(a, b):
    return jnp.dot(a, b, preferred_element_type=F32)


def np_split(table):
    hi = table.astype(ml_dtypes.bfloat16)
    lo = (table - hi.astype(np.float64)).astype(ml_dtypes.bfloat16)
    return hi, lo


def split(x):
    hi = x.astype(BF16).astype(F32)
    return hi, x - hi


def stack_three(x):
    hi, lo = split(x)
    return jnp.concatenate([hi, lo, hi], axis=0).astype(BF16)


def np_three(table):
    hi, lo = np_split(table)
    return np.concatenate([hi, hi, lo], axis=1)


def np_tables(grid, zmodes):
    freqs = np.concatenate([np.arange(MX), grid - MX + np.arange(MX)])
    cells = np.arange(grid)
    ang = 2.0 * math.pi / grid * (freqs[:, None] * cells[None, :] % grid)
    half = 2.0 * math.pi / grid * (freqs[:, None] * (2 * np.arange(grid // 2))[None, :] % grid)
    tw = 2.0 * math.pi / grid * freqs
    count = freqs.size
    fwd_x = np.concatenate([np.cos(ang), -np.sin(ang)], axis=0)
    hi, lo = np_split(fwd_x)
    fwd_x_two = np.concatenate([hi, lo], axis=0)
    fwd_x_three = np_three(fwd_x)
    fwd_y = np_three(np.concatenate([np.cos(half), np.sin(half)], axis=0))
    inv_y = np_three(np.concatenate([np.cos(half.T), np.sin(half.T)], axis=0))
    inv_x = np_three(np.concatenate([np.cos(ang.T), -np.sin(ang.T)], axis=1))
    tw_c = np.ones((count, LANES), np.float32)
    tw_s = np.zeros((count, LANES), np.float32)
    tw_c[:, LANES // 2:] = np.cos(tw)[:, None]
    tw_s[:, LANES // 2:] = np.sin(tw)[:, None]
    kz = np.zeros((ROWS,), np.int64)
    kz[:zmodes] = np.arange(zmodes)
    zang = 2.0 * math.pi / grid * (cells[:, None] * kz[None, :] % grid)
    z_c = np.cos(zang).astype(np.float32)
    z_s = np.sin(zang).astype(np.float32)
    scale = (np.where(kz == 0, 1.0, 2.0) / float(grid**3)).astype(np.float32)
    return dict(fwd_x_two=fwd_x_two, fwd_x_three=fwd_x_three, fwd_y=fwd_y, inv_y=inv_y,
                inv_x=inv_x, tw_c=tw_c, tw_s=tw_s, z_c=z_c, z_s=z_s, scale=scale)


def low_half(shape):
    return lax.broadcasted_iota(jnp.int32, shape, len(shape) - 1) % LANES < LANES // 2


def roll_half(x):
    return pltpu.roll(x, LANES // 2, x.ndim - 1)


def put_rows(g_ref, chunk, first, half):
    for r in range(0, chunk.shape[0], 8):
        for j in range(chunk.shape[1] // LANES):
            g_ref[pl.ds(r * half + first + j, 8, stride=half), :] = chunk[r:r + 8, j * LANES:(j + 1) * LANES]


def get_rows(n_ref, first, blocks, rows, half):
    cols = []
    for j in range(blocks):
        cols.append(jnp.concatenate(
            [n_ref[pl.ds(r * half + first + j, 8, stride=half), :] for r in range(0, rows, 8)], axis=0))
    return jnp.concatenate(cols, axis=1)


def fwd_yz(g_ref, acc_ref, fy, twc, tws, zc_ref, zs_ref, z, zmodes, half):
    count = 2 * MX
    low = low_half((count, LANES))
    sign = jnp.where(low, 1.0, -1.0).astype(F32)
    cs = [zc_ref[z, k] for k in range(zmodes)]
    sn = [zs_ref[z, k] for k in range(zmodes)]
    for a in range(count):
        g = jnp.concatenate([g_ref[a * half:(a + 1) * half, :],
                             g_ref[(count + a) * half:(count + a + 1) * half, :]], axis=1)
        h = mm(fy, stack_three(g))
        re = h[:count, :LANES] + h[count:, LANES:]
        im = h[:count, LANES:] - h[count:, :LANES]
        re2 = re * twc + im * tws
        im2 = im * twc - re * tws
        row = jnp.where(low, re2 + roll_half(re2), im2 + roll_half(im2))
        turned = sign * roll_half(row)
        for k in range(zmodes):
            acc_ref[k, a * count:(a + 1) * count, :] += cs[k] * row + sn[k] * turned


def give_modes(acc_ref, out_ref, zmodes):
    pairs = acc_ref.shape[1]
    for k in range(zmodes):
        out_ref[pl.ds(k, pairs, stride=ROWS), :] = acc_ref[k]
    for k in range(zmodes, ROWS):
        out_ref[pl.ds(k, pairs, stride=ROWS), :] = jnp.zeros((pairs, LANES), F32)


def take_modes(m_ref, scr, zmodes):
    pairs = scr.shape[1]
    for k in range(zmodes):
        scr[k] = m_ref[pl.ds(k, pairs, stride=ROWS), :]


def inv_zy(scr, n_ref, iy, twc, tws, zc_ref, zs_ref, z, zmodes, half):
    count = 2 * MX
    low = low_half((count, LANES))
    sign = jnp.where(low, -1.0, 1.0).astype(F32)
    cs = [zc_ref[z, k] for k in range(zmodes)]
    sn = [zs_ref[z, k] for k in range(zmodes)]
    for a in range(count):
        part = scr[0, a * count:(a + 1) * count, :]
        first, second = cs[0] * part, sn[0] * part
        for k in range(1, zmodes):
            part = scr[k, a * count:(a + 1) * count, :]
            first += cs[k] * part
            second += sn[k] * part
        line = first + sign * roll_half(second)
        other = roll_half(line)
        re = jnp.where(low, line, other)
        im = jnp.where(low, other, line)
        p_re = re * twc - im * tws
        p_im = im * twc + re * tws
        o = mm(iy, stack_three(jnp.concatenate([p_re, p_im], axis=1)))
        n_ref[a * half:(a + 1) * half, :] = o[:half, :LANES] - o[half:, LANES:]
        n_ref[(count + a) * half:(count + a + 1) * half, :] = o[:half, LANES:] + o[half:, :LANES]


def forward_kernel(zmodes, half, zc_ref, zs_ref, x_ref, fx_ref, fy_ref, twc_ref, tws_ref, out_ref, acc_ref, g_ref):
    z = pl.program_id(0)

    @pl.when(z == 0)
    def _():
        acc_ref[...] = jnp.zeros_like(acc_ref)

    rows = 4 * MX
    for n in range(0, x_ref.shape[3], WIDE):
        u = mm(fx_ref[...], x_ref[0, 0, :, n:n + WIDE])
        put_rows(g_ref, u[:rows] + u[rows:], n // LANES, half)
    fwd_yz(g_ref, acc_ref, fy_ref[...], twc_ref[...], tws_ref[...], zc_ref, zs_ref, z, zmodes, half)

    @pl.when(z == pl.num_programs(0) - 1)
    def _():
        give_modes(acc_ref, out_ref, zmodes)


def middle_kernel(zmodes, half, ic_ref, is_ref, fc_ref, fs_ref, m_ref, x_ref, ct_ref, w_ref, b_ref,
                  iy_ref, ix_ref, fx_ref, fy_ref, twc_ref, tws_ref,
                  out_ref, slope_ref, modes_ref, scr, acc_ref, n_ref, g_ref):
    z = pl.program_id(0)

    @pl.when(z == 0)
    def _():
        acc_ref[...] = jnp.zeros_like(acc_ref)
        take_modes(m_ref, scr, zmodes)

    twc, tws = twc_ref[...], tws_ref[...]
    inv_zy(scr, n_ref, iy_ref[...], twc, tws, ic_ref, is_ref, z, zmodes, half)
    rate = math.sqrt(2.0 / math.pi)
    for n in range(0, x_ref.shape[3], WIDE):
        cols = get_rows(n_ref, n // LANES, WIDE // LANES, 4 * MX, half)
        spectral = mm(ix_ref[...], stack_three(cols))
        u = spectral + mm(x_ref[0, 0, :, n:n + WIDE], w_ref[...]) + b_ref[...]
        square = u * u
        t = jnp.tanh(rate * u * (1.0 + 0.044715 * square))
        gate = 0.5 * (1.0 + t)
        out_ref[0, 0, :, n:n + WIDE] = (u * gate).astype(BF16)
        rise = gate + 0.5 * u * (1.0 - t * t) * (rate * (1.0 + 3.0 * 0.044715 * square))
        slope = ct_ref[0, 0, :, n:n + WIDE].astype(F32) * rise
        slope_ref[0, :, n:n + WIDE] = slope
        put_rows(g_ref, mm(fx_ref[...], stack_three(slope)), n // LANES, half)
    fwd_yz(g_ref, acc_ref, fy_ref[...], twc, tws, fc_ref, fs_ref, z, zmodes, half)

    @pl.when(z == pl.num_programs(0) - 1)
    def _():
        give_modes(acc_ref, modes_ref, zmodes)


def final_kernel(zmodes, half, ic_ref, is_ref, m_ref, slope_ref, w_ref, iy_ref, ix_ref, twc_ref, tws_ref,
                 out_ref, scr, n_ref):
    z = pl.program_id(0)

    @pl.when(z == 0)
    def _():
        take_modes(m_ref, scr, zmodes)

    inv_zy(scr, n_ref, iy_ref[...], twc_ref[...], tws_ref[...], ic_ref, is_ref, z, zmodes, half)
    for n in range(0, slope_ref.shape[2], WIDE):
        cols = get_rows(n_ref, n // LANES, WIDE // LANES, 4 * MX, half)
        total = mm(ix_ref[...], stack_three(cols))
        hi, lo = split(slope_ref[0, :, n:n + WIDE])
        total += mm(hi.astype(BF16), w_ref[...]) + mm(lo.astype(BF16), w_ref[...])
        out_ref[0, 0, :, n:n + WIDE] = total.astype(BF16)


def halves(v):
    low = low_half(v.shape)
    other = roll_half(v)
    return jnp.where(low, v, other), jnp.where(low, other, v)


def mix_kernel(zmodes, recv_ref, w_ref, e_ref, spec_ref, out_ref):
    block = spec_ref.shape[0]
    v = recv_ref[0]
    for s in range(1, recv_ref.shape[0]):
        v += recv_ref[s]
    spec_ref[...] = v
    flat = v.reshape(block * ROWS, LANES)
    both = jnp.concatenate(halves(flat), axis=0)
    hi, lo = split(both)
    left = jnp.where(low_half(both.shape), hi, lo).astype(BF16)
    sum_re = jnp.zeros((block, zmodes, WIDE), F32)
    sum_im = jnp.zeros((block, zmodes, WIDE), F32)
    rows = block * ROWS
    for n in range(0, w_ref.shape[3], WIDE):
        x = mm(left, e_ref[:, n:n + WIDE])
        x_re = x[:rows].reshape(block, ROWS, WIDE)[:, :zmodes]
        x_im = x[rows:].reshape(block, ROWS, WIDE)[:, :zmodes]
        w_re = w_ref[0, :, :, n:n + WIDE].astype(F32)
        w_im = w_ref[1, :, :, n:n + WIDE].astype(F32)
        sum_re += x_re * w_re - x_im * w_im
        sum_im += x_re * w_im + x_im * w_re
    half_re = sum_re[..., :LANES] + sum_re[..., LANES:]
    half_im = sum_im[..., :LANES] + sum_im[..., LANES:]
    half_re += roll_half(half_re)
    half_im += roll_half(half_im)
    out_ref[...] = jnp.zeros_like(out_ref)
    out_ref[:, :zmodes, :] = jnp.where(low_half(half_re.shape), half_re, half_im)


def back_kernel(zmodes, recv_ref, w_ref, f_ref, spec_ref, out_ref, p_ref):
    block = spec_ref.shape[0]
    v = recv_ref[0]
    for s in range(1, recv_ref.shape[0]):
        v += recv_ref[s]
    spec_ref[...] = v
    c_re, c_im = halves(v)
    c_re = jnp.concatenate([c_re, c_re], axis=2)[:, :zmodes]
    c_im = jnp.concatenate([c_im, c_im], axis=2)[:, :zmodes]
    p_ref[...] = jnp.zeros_like(p_ref)
    rows = block * ROWS
    total = jnp.zeros((4 * rows, LANES), F32)
    for n in range(0, w_ref.shape[3], WIDE):
        w_re = w_ref[0, :, :, n:n + WIDE].astype(F32)
        w_im = w_ref[1, :, :, n:n + WIDE].astype(F32)
        slot = n // WIDE % 2
        p_ref[slot, 0, :, :zmodes, :] = c_re * w_re + c_im * w_im
        p_ref[slot, 1, :, :zmodes, :] = c_im * w_re - c_re * w_im
        hi, lo = split(p_ref[slot].reshape(2 * rows, WIDE))
        total += mm(jnp.concatenate([hi, lo], axis=0).astype(BF16), f_ref[n:n + WIDE, :])
    total = total[:2 * rows] + total[2 * rows:]
    both = jnp.where(low_half((rows, LANES)), total[:rows], total[rows:])
    out_ref[...] = both.reshape(block, ROWS, LANES)


def grads_kernel(zmodes, samples, stride, v_ref, c_ref, out_ref, x_ref):
    block = out_ref.shape[1]
    chan = LANES // 2
    low = low_half((ROWS, LANES))
    sign = jnp.where(low_half((samples, LANES)), 1.0, -1.0).astype(F32)
    base = pl.program_id(0) * block * ROWS
    for q in range(block):
        slot = q % 2
        for k in range(zmodes):
            at = pl.ds(base + (q * ROWS + k), samples, stride=stride)
            a = v_ref[at, :]
            b = c_ref[at, :]
            left = jnp.concatenate([a, roll_half(a)], axis=0)
            right = jnp.concatenate([b, sign * roll_half(b)], axis=0)
            l_hi, l_lo = split(left)
            r_hi, r_lo = split(right)
            lhs = jnp.concatenate([l_hi, l_lo, l_hi], axis=0).astype(BF16)[:, :chan]
            rhs = jnp.concatenate([r_hi, r_hi, r_lo], axis=0).astype(BF16)
            x_ref[slot, k * chan:(k + 1) * chan, :] = lax.dot_general(
                lhs, rhs, (((0,), (0,)), ((), ())), preferred_element_type=F32)
        for j in range(chan // 2):
            even = x_ref[slot, pl.ds(2 * j, ROWS, stride=chan), :]
            odd = x_ref[slot, pl.ds(2 * j + 1, ROWS, stride=chan), :]
            lanes = slice(j * LANES, (j + 1) * LANES)
            out_ref[0, q, :, lanes] = jnp.where(low, even, roll_half(odd))[:zmodes]
            out_ref[1, q, :, lanes] = jnp.where(low, roll_half(even), odd)[:zmodes]


def whole(a):
    rank = a.ndim
    return pl.BlockSpec(a.shape, lambda i: (0,) * rank)


SMEM = pl.BlockSpec(memory_space=pltpu.SMEM)


def on_device(parts, inputs, cotangent, mode_weights, local_weight, local_bias):
    _, planes, grid, width = inputs.shape
    chan = local_weight.shape[0]
    pairs_here, zmodes, entries = mode_weights.shape[1:]
    pairs = pairs_here * parts
    half = grid // 2
    tab = np_tables(grid, zmodes)
    const = {name: jnp.asarray(t) for name, t in tab.items()}
    first = lax.axis_index("mp") * planes
    z_c = lax.dynamic_slice_in_dim(const["z_c"], first, planes, 0)
    z_s = lax.dynamic_slice_in_dim(const["z_s"], first, planes, 0)
    zsc_c, zsc_s = z_c * const["scale"], z_s * const["scale"]
    params = pltpu.CompilerParams(**PARAMS)
    plane = pl.BlockSpec((1, 1, grid, width), lambda z: (0, z, 0, 0))
    flat = pl.BlockSpec((1, grid, width), lambda z: (z, 0, 0))
    modes_shape = jax.ShapeDtypeStruct((pairs * ROWS, LANES), F32)
    modes_spec = pl.BlockSpec((pairs * ROWS, LANES), lambda z: (0, 0))
    acc = pltpu.VMEM((zmodes, pairs, LANES), F32)
    lines = pltpu.VMEM((4 * MX * half, LANES), F32)
    fy, iy, ix, twc, tws = (const[n] for n in ("fwd_y", "inv_y", "inv_x", "tw_c", "tw_s"))
    fx2, fx3 = const["fwd_x_two"], const["fwd_x_three"]

    def exchange(x):
        return lax.all_to_all(x.reshape(parts, pairs_here, ROWS, LANES), "mp", 0, 0)

    def spread(x):
        every = jnp.broadcast_to(x[None], (parts,) + x.shape)
        return lax.all_to_all(every, "mp", 0, 0).reshape(pairs * ROWS, LANES)

    partial = pl.pallas_call(
        functools.partial(forward_kernel, zmodes, half),
        grid=(planes,),
        in_specs=[SMEM, SMEM, plane, whole(fx2), whole(fy), whole(twc), whole(tws)],
        out_specs=modes_spec, out_shape=modes_shape, scratch_shapes=[acc, lines],
        compiler_params=params, name="forward",
    )(z_c, z_s, inputs, fx2, fy, twc, tws)

    block = 8
    recv_spec = pl.BlockSpec((parts, block, ROWS, LANES), lambda i: (0, i, 0, 0))
    w_spec = pl.BlockSpec((2, block, zmodes, entries), lambda i: (0, i, 0, 0))
    m_spec = pl.BlockSpec((block, ROWS, LANES), lambda i: (i, 0, 0))
    m_shape = jax.ShapeDtypeStruct((pairs_here, ROWS, LANES), F32)
    eye = np.eye(chan, dtype=np.float32)
    expand = np.concatenate([np.repeat(eye, chan, axis=1)] * 2, axis=0)
    fold = np.repeat(np.concatenate([eye, eye], axis=1), chan, axis=0)
    expand, fold = jnp.asarray(expand, BF16), jnp.asarray(fold, BF16)
    spectrum, mixed = pl.pallas_call(
        functools.partial(mix_kernel, zmodes),
        grid=(pairs_here // block,),
        in_specs=[recv_spec, w_spec, whole(expand)],
        out_specs=[m_spec, m_spec], out_shape=[m_shape, m_shape],
        compiler_params=params, name="mix",
    )(exchange(partial), mode_weights, expand)
    all_spectra = lax.all_gather(spectrum, "dp")

    repeat = WIDE // chan
    eyes = jnp.eye(repeat, dtype=BF16)
    w_wide = jnp.kron(eyes, local_weight)
    wt_wide = jnp.kron(eyes, local_weight.T)
    bias = jnp.tile(local_bias, repeat)[None, :]
    outputs, slope, cot_partial = pl.pallas_call(
        functools.partial(middle_kernel, zmodes, half),
        grid=(planes,),
        in_specs=[SMEM] * 4 + [modes_spec, plane, plane, whole(w_wide), whole(bias), whole(iy), whole(ix),
                               whole(fx3), whole(fy), whole(twc), whole(tws)],
        out_specs=[plane, flat, modes_spec],
        out_shape=[jax.ShapeDtypeStruct(inputs.shape, BF16),
                   jax.ShapeDtypeStruct((planes, grid, width), F32), modes_shape],
        scratch_shapes=[acc, acc, lines, lines],
        compiler_params=params, name="middle",
    )(zsc_c, zsc_s, zsc_c, zsc_s, spread(mixed), inputs, cotangent, w_wide, bias, iy, ix, fx3, fy, twc, tws)

    cot_spectrum, back = pl.pallas_call(
        functools.partial(back_kernel, zmodes),
        grid=(pairs_here // block,),
        in_specs=[recv_spec, w_spec, whole(fold)],
        out_specs=[m_spec, m_spec], out_shape=[m_shape, m_shape],
        scratch_shapes=[pltpu.VMEM((2, 2, block, ROWS, WIDE), F32)],
        compiler_params=params, name="back",
    )(exchange(cot_partial), mode_weights, fold)
    all_cots = lax.all_gather(cot_spectrum, "dp")

    input_grads = pl.pallas_call(
        functools.partial(final_kernel, zmodes, half),
        grid=(planes,),
        in_specs=[SMEM] * 2 + [modes_spec, flat, whole(wt_wide), whole(iy), whole(ix), whole(twc), whole(tws)],
        out_specs=plane, out_shape=jax.ShapeDtypeStruct(inputs.shape, BF16),
        scratch_shapes=[acc, lines],
        compiler_params=params, name="final",
    )(z_c, z_s, spread(back), slope, wt_wide, iy, ix, twc, tws)

    samples = all_spectra.shape[0]
    stride = pairs_here * ROWS
    gathered = pl.BlockSpec((samples * stride, LANES), lambda i: (0, 0))
    group = 4
    mode_grads = pl.pallas_call(
        functools.partial(grads_kernel, zmodes, samples, stride),
        grid=(pairs_here // group,),
        in_specs=[gathered, gathered],
        out_specs=pl.BlockSpec((2, group, zmodes, entries), lambda i: (0, i, 0, 0)),
        out_shape=jax.ShapeDtypeStruct((2, pairs_here, zmodes, entries), F32),
        scratch_shapes=[pltpu.VMEM((2, ROWS * chan, LANES), F32)],
        compiler_params=params, name="grads",
    )(all_spectra.reshape(samples * stride, LANES), all_cots.reshape(samples * stride, LANES))
    return (outputs, input_grads, mode_grads)


def solution(mesh):
    field = P("dp", "mp", None, None)
    weights = P(None, "mp", None, None)
    return jax.shard_map(
        functools.partial(on_device, mesh.shape["mp"]),
        mesh=mesh,
        in_specs=(field, field, weights, P(), P()),
        out_specs=(field, field, weights),
        check_vma=False,
    )
```

time: 718 us -> 230 us (0.32)
  matrix products: 266 us -> 0 us
  local copies, waits for them, and re-layouts: 199 us -> 37.5 us
  waiting for transfers between devices: 169 us -> 26.6 us
  Pallas kernels: 0 us -> 120 us
  other arithmetic: 39.8 us -> 1.03 us
  blocking collectives: 0 us -> 16.1 us
  starting transfers between devices: 28.1 us -> 12.4 us
    dot_general x50 -> x0, matrix products: 266 us -> none  [the longest x2 30.1 us: inverse_xy(): jnp.einsum('ax,szayc->szxyc', sin_xy, middle_imag, precision=highest)]
    psum x1 -> x0, waiting for transfers between devices: 164 us -> none  [on_device(): summed = lax.psum(mode_terms(spectra, cot_spectra, chan), 'dp')]
    pallas_call x0 -> x6, Pallas kernels: none -> 120 us  [the longest x1 46.8 us: on_device(): pl.pallas_call(functools.partial(middle_kernel, zmodes, half), grid=(plan...]
    reshape x9 -> x0, local copies, waits for them, and re-layouts: 99.9 us -> none  [the longest x2 25.3 us: inverse_xy(): return field.reshape(samples, planes, grid, grid * chan)]
    sub x2 -> x0, local copies, waits for them, and re-layouts: 28.7 us -> none  [inverse_xy(): jnp.einsum('ax,szayc->szxyc', cos_xy, middle_real, precision=highest)]
    unnamed x59 -> x32, local copies, waits for them, and re-layouts: 12.6 us -> 34.8 us
    squeeze x2 -> x0, local copies, waits for them, and re-layouts: 22.1 us -> none  [the longest x1 11.1 us: on_device(): weight_real = weights[0]]
    another operation x9 -> x2, local copies, waits for them, and re-layouts: 21.6 us -> 0.08 us  [on_device(): bias = jnp.tile(local_bias, repeat)[None, :]]
  transfers between devices with their start and end apart: 5 -> 5, of which waited for: 2 -> 3; matrix products, arithmetic and copies ran while one was open for 28% -> 6% of each run, Pallas kernels for 0% -> 32%
where the time goes in v1:
time: 230 us; the launch traced here: 228 us
  Pallas kernels  120 us (52%)
  local copies, waits for them, and re-layouts  37.5 us (16%)
  waiting for transfers between devices  26.6 us (12%)
  blocking collectives  16.1 us (7%)
  between operations  14.2 us (6%)
  starting transfers between devices  12.4 us (5%)
    pallas_call x1, Pallas kernels, on_device(): pl.pallas_call(functools.partial(middle_kernel, zmodes, half), grid=(plan...  46.8 us
    unnamed x32, local copies, waits for them, and re-layouts  34.8 us
    pallas_call x1, Pallas kernels, on_device(): pl.pallas_call(functools.partial(grads_kernel, zmodes, samples, stride),...  25.4 us
    all_to_all x2, waiting for transfers between devices, spread(): return lax.all_to_all(every, 'mp', 0, 0).reshape(pairs * ROWS, LANES)  23.6 us
    pallas_call x1, Pallas kernels, on_device(): pl.pallas_call(functools.partial(final_kernel, zmodes, half), grid=(plane...  16.6 us
    all_to_all x1, blocking collectives, exchange(): return lax.all_to_all(x.reshape(parts, pairs_here, ROWS, LANES), 'mp', 0, 0)  16.1 us
    pallas_call x1, Pallas kernels, on_device(): pl.pallas_call(functools.partial(forward_kernel, zmodes, half), grid=(pla...  12.1 us
    pallas_call x1, Pallas kernels, on_device(): pl.pallas_call(functools.partial(back_kernel, zmodes), grid=(pairs_here /...  10.4 us
  transfers between devices with their start and end apart: 5, of which 3 were waited for; matrix products, arithmetic and copies ran while one was open for 6% of the time, Pallas kernels for 32%

profile of v1, /device:TPU:0, one launch (start us, length us, event | category | flops | bytes accessed | tf_op | source)
XLA Modules:
  0.0 228.4 jit_solution(15527270001718195520)
XLA Ops:
  7.2 0.8 constant_dynamic-slice_fusion
  7.9 0.0 copy-start.3
  7.9 0.7 copy-done.3
  8.6 0.0 copy-start.5
  8.6 0.7 copy-done.5
  9.3 0.0 copy-start.9
  9.3 0.7 copy-done.9
  10.0 0.0 copy-start.12
  10.0 0.7 copy-done.12
  10.7 12.1 %forward.1 = f32[2048,128]{1,0:T(8,128)} custom-call(f32[12,8]{1,0:T(8,128)S(1)} %get-tuple-element.30.zc_ref.ic_ref, f32[12,8]{1,0:T(8,128)S(1)} %get-tuple-element.23.zs_ref.is_ref, bf16[1,12,48,3072]{3,2,1,0:T(8,128)(2,1)} %x_ref.3, bf16[64,48]{1,0:T(8,128)(2,1)S(1)} %copy-done.12, bf16[32,72]{1,0:T(8,128)(2,1)S(1)} %copy-done.9, ...), custom_call_target="tpu_custom_call" | custom-call | tf_op jit(solution)/shard_map/forward/pallas_call | solution.py:347
  22.8 5.2 %all-to-all-start = ((f32[4,64,8,128]{3,2,1,0:T(8,128)}), f32[4,64,8,128]{3,2,1,0:T(8,128)S(1)}, u32[]{:S(2)}, u32[]{:S(2)}) async-start(f32[4,64,8,128]{3,2,1,0:T(8,128)} %bitcast), calls=%async_computation | async-start | bytes 2097152 | tf_op jit(solution)/shard_map/all_to_all | solution.py:341
  28.0 0.0 copy-start.2
  28.0 0.0 all-gather.5.cloned.1.call-start
  28.0 10.6 %copy.24.w_ref = bf16[2,64,7,4096]{3,2,1,0:T(8,128)(2,1)} copy(bf16[2,64,7,4096]{3,1,2,0:T(8,128)(2,1)} %param.19) | data formatting | bytes 14680064 | tf_op args[2]
  38.6 3.0 %all-to-all-done.recv_ref = f32[4,64,8,128]{3,2,1,0:T(8,128)S(1)} async-done(((f32[4,64,8,128]{3,2,1,0:T(8,128)}), f32[4,64,8,128]{3,2,1,0:T(8,128)S(1)}, u32[]{:S(2)}, u32[]{:S(2)}) %all-to-all-start) | async-done | bytes 1048608 | tf_op jit(solution)/shard_map/all_to_all | solution.py:341
  41.6 0.0 copy-done.2
  41.6 9.3 %mix.1 = (f32[64,8,128]{2,1,0:T(8,128)}, f32[64,8,128]{2,1,0:T(8,128)S(1)}) custom-call(f32[4,64,8,128]{3,2,1,0:T(8,128)S(1)} %all-to-all-done.recv_ref, bf16[2,64,7,4096]{3,2,1,0:T(8,128)(2,1)} %copy.24.w_ref, bf16[128,4096]{1,0:T(8,128)(2,1)S(1)} %copy-done.2), custom_call_target="tpu_custom_call" | custom-call | tf_op jit(solution)/shard_map/mix/pallas_call | solution.py:364
  50.9 0.0 copy-start.14
  50.9 0.0 copy-start.13
  50.9 0.0 copy-start.4
  50.9 0.0 copy-start.6
  50.9 0.0 copy-start.7
  51.0 0.0 copy-start.8
  51.0 0.0 copy-start.10
  51.0 0.0 copy-start.11
  51.0 0.0 all-gather.5.cloned.1.call-update
  51.0 1.0 broadcast_in_dim.10
  52.1 3.5 %all-to-all-start.1 = ((f32[4,64,8,128]{3,2,1,0:T(8,128)}), f32[4,64,8,128]{3,2,1,0:T(8,128)S(1)}, u32[]{:S(2)}, u32[]{:S(2)}) async-start(f32[4,64,8,128]{3,2,1,0:T(8,128)} %broadcast_in_dim.10), calls=%async_computation.1 | async-start | bytes 2097152 | tf_op jit(solution)/shard_map/all_to_all | solution.py:345
  55.6 0.0 all-gather.7.cloned.1.call-start
  55.6 0.0 copy-done.14
  55.7 0.1 broadcast_in_dim_tile.3.b_ref
  55.7 0.0 copy-done.13
  55.7 0.1 copy.26
  55.8 0.3 broadcast_multiply_fusion
  56.1 0.2 mul.65.w_ref
  56.3 12.3 %all-to-all-done.1 = f32[4,64,8,128]{3,2,1,0:T(8,128)S(1)} async-done(((f32[4,64,8,128]{3,2,1,0:T(8,128)}), f32[4,64,8,128]{3,2,1,0:T(8,128)S(1)}, u32[]{:S(2)}, u32[]{:S(2)}) %all-to-all-start.1) | async-done | bytes 1048608 | tf_op jit(solution)/shard_map/all_to_all | solution.py:345
  68.7 0.0 copy-done.4
  68.7 0.0 copy-done.6
  68.7 0.0 copy-done.7
  68.7 0.0 copy-done.8
  68.7 0.0 copy-done.10
  68.7 0.0 copy-done.11
  68.7 0.0 copy-start.1
  68.7 46.8 %middle.1 = (bf16[1,12,48,3072]{3,2,1,0:T(8,128)(2,1)}, f32[12,48,3072]{2,1,0:T(8,128)}, f32[2048,128]{1,0:T(8,128)S(1)}) custom-call(f32[12,8]{1,0:T(8,128)S(1)} %get-tuple-element.29.ic_ref.fc_ref, f32[12,8]{1,0:T(8,128)S(1)} %get-tuple-element.24.is_ref.fs_ref, f32[12,8]{1,0:T(8,128)S(1)} %get-tuple-element.29.ic_ref.fc_ref, ...), custom_call_target="tpu_custom_call" | custom-call | tf_op jit(solution)/shard_map/middle/pallas_call | solution.py:378
  115.5 16.1 %all_to_all.20.recv_ref = f32[4,64,8,128]{3,2,1,0:T(8,128)S(1)} all-to-all(f32[4,64,8,128]{3,2,1,0:T(8,128)S(1)} %bitcast.10), channel_id=1, replica_groups=mesh['dp'=8,'mp'=4] {'mp'}, dimensions={0} | all-to-all | bytes 2097152 | tf_op jit(solution)/shard_map/all_to_all | solution.py:341
  131.6 0.0 copy-done.1
  131.6 10.4 %back.1 = (f32[64,8,128]{2,1,0:T(8,128)}, f32[64,8,128]{2,1,0:T(8,128)S(1)}) custom-call(f32[4,64,8,128]{3,2,1,0:T(8,128)S(1)} %all_to_all.20.recv_ref, bf16[2,64,7,4096]{3,2,1,0:T(8,128)(2,1)} %copy.24.w_ref, bf16[4096,128]{1,0:T(8,128)(2,1)S(1)} %copy-done.1), custom_call_target="tpu_custom_call" | custom-call | tf_op jit(solution)/shard_map/back/pallas_call | solution.py:390
  142.0 0.0 all-gather.7.cloned.1.call-update
  142.0 1.0 broadcast_in_dim.11
  143.1 3.7 %all-to-all-start.3 = ((f32[4,64,8,128]{3,2,1,0:T(8,128)}), f32[4,64,8,128]{3,2,1,0:T(8,128)S(1)}, u32[]{:S(2)}, u32[]{:S(2)}) async-start(f32[4,64,8,128]{3,2,1,0:T(8,128)} %broadcast_in_dim.11), calls=%async_computation.3 | async-start | bytes 2097152 | tf_op jit(solution)/shard_map/all_to_all | solution.py:345
  146.8 0.2 mul.68.w_ref
  147.0 11.2 %all-to-all-done.3 = f32[4,64,8,128]{3,2,1,0:T(8,128)S(1)} async-done(((f32[4,64,8,128]{3,2,1,0:T(8,128)}), f32[4,64,8,128]{3,2,1,0:T(8,128)S(1)}, u32[]{:S(2)}, u32[]{:S(2)}) %all-to-all-start.3) | async-done | bytes 1048608 | tf_op jit(solution)/shard_map/all_to_all | solution.py:345
  158.2 16.6 %final.1 = bf16[1,12,48,3072]{3,2,1,0:T(8,128)(2,1)} custom-call(f32[12,8]{1,0:T(8,128)S(1)} %get-tuple-element.30.zc_ref.ic_ref, f32[12,8]{1,0:T(8,128)S(1)} %get-tuple-element.23.zs_ref.is_ref, f32[2048,128]{1,0:T(8,128)S(1)} %bitcast.8, f32[12,48,3072]{2,1,0:T(8,128)} %get-tuple-element.14.slope_ref, bf16[256,256]{1,0:T(8,128)(2,1)S(1)} %mul.68.w_ref, ...), custom_call_target="tpu_custom_call" | custom-call | tf_op jit(solution)/shard_map/final/pallas_call | solution.py:400
  174.8 0.0 all-gather.5.cloned.1.call-done
  174.8 0.0 all-gather.7.cloned.1.call-done
  174.8 0.0 copy-start
  174.8 1.6 copy-done
  176.4 25.4 %grads.1 = f32[2,64,7,4096]{3,2,1,0:T(8,128)} custom-call(f32[4096,128]{1,0:T(8,128)S(1)} %bitcast.9, f32[4096,128]{1,0:T(8,128)} %bitcast.11), custom_call_target="tpu_custom_call" | custom-call | tf_op jit(solution)/shard_map/grads/pallas_call | solution.py:413
  201.8 19.7 %copy.27 = f32[2,64,7,4096]{3,1,2,0:T(8,128)} copy(f32[2,64,7,4096]{3,2,1,0:T(8,128)} %grads.1) | data formatting | bytes 29360128
  (2 shorter events, 0.0 us)
Async XLA Ops:
  7.9 0.7 copy-start.3
  8.6 0.7 copy-start.5
  9.3 0.7 copy-start.9
  10.0 0.7 copy-start.12
  22.8 18.8 %all-to-all-start = ((f32[4,64,8,128]{3,2,1,0:T(8,128)}), f32[4,64,8,128]{3,2,1,0:T(8,128)S(1)}, u32[]{:S(2)}, u32[]{:S(2)}) async-start(f32[4,64,8,128]{3,2,1,0:T(8,128)} %bitcast), calls=%async_computation | async-start | bytes 2097152 | tf_op jit(solution)/shard_map/all_to_all | solution.py:341
  28.0 13.6 %copy-start.2 = (bf16[128,4096]{1,0:T(8,128)(2,1)S(1)}, bf16[128,4096]{1,0:T(8,128)(2,1)}, u32[]{:S(2)}) copy-start(bf16[128,4096]{1,0:T(8,128)(2,1)} %constant.44.clone.e_ref) | copy-start | bytes 3145732
  28.0 146.8 %all-gather.5.cloned.1.call-start = ((), (), s32[]{:S(2)}) async-start(), calls=%async_computation.4 | async-start | bytes 2359296 | tf_op jit(solution)/shard_map/all_gather | solution.py:371
  50.9 4.7 %copy-start.14 = (f32[64]{0:T(128)S(1)}, f32[64]{0:T(128)}, u32[]{:S(2)}) copy-start(f32[64]{0:T(128)} %param.21) | copy-start | bytes 772
  50.9 4.8 %copy-start.13 = (bf16[64,64]{1,0:T(8,128)(2,1)S(1)}, bf16[64,64]{1,0:T(8,128)(2,1)}, u32[]{:S(2)}) copy-start(bf16[64,64]{1,0:T(8,128)(2,1)} %param.20) | copy-start | bytes 24580
  50.9 17.7 %copy-start.4 = (f32[16,128]{1,0:T(8,128)S(1)}, f32[16,128]{1,0:T(8,128)}, u32[]{:S(2)}) copy-start(f32[16,128]{1,0:T(8,128)} %constant.40.clone.tws_ref) | copy-start | bytes 24580
  50.9 17.7 %copy-start.6 = (f32[16,128]{1,0:T(8,128)S(1)}, f32[16,128]{1,0:T(8,128)}, u32[]{:S(2)}) copy-start(f32[16,128]{1,0:T(8,128)} %constant.39.clone.twc_ref) | copy-start | bytes 24580
  50.9 17.7 %copy-start.7 = (bf16[48,96]{1,0:T(8,128)(2,1)S(1)}, bf16[48,96]{1,0:T(8,128)(2,1)}, u32[]{:S(2)}) copy-start(bf16[48,96]{1,0:T(8,128)(2,1)} %constant.38.clone.ix_ref) | copy-start | bytes 27652
  51.0 17.7 %copy-start.8 = (bf16[48,48]{1,0:T(8,128)(2,1)S(1)}, bf16[48,48]{1,0:T(8,128)(2,1)}, u32[]{:S(2)}) copy-start(bf16[48,48]{1,0:T(8,128)(2,1)} %constant.37.clone.iy_ref) | copy-start | bytes 13828
  51.0 17.7 %copy-start.10 = (bf16[32,72]{1,0:T(8,128)(2,1)S(1)}, bf16[32,72]{1,0:T(8,128)(2,1)}, u32[]{:S(2)}) copy-start(bf16[32,72]{1,0:T(8,128)(2,1)} %constant.36.clone.fy_ref) | copy-start | bytes 13828
  51.0 17.7 %copy-start.11 = (bf16[32,144]{1,0:T(8,128)(2,1)S(1)}, bf16[32,144]{1,0:T(8,128)(2,1)}, u32[]{:S(2)}) copy-start(bf16[32,144]{1,0:T(8,128)(2,1)} %constant.35.clone.fx_ref) | copy-start | bytes 27652
  52.1 16.6 %all-to-all-start.1 = ((f32[4,64,8,128]{3,2,1,0:T(8,128)}), f32[4,64,8,128]{3,2,1,0:T(8,128)S(1)}, u32[]{:S(2)}, u32[]{:S(2)}) async-start(f32[4,64,8,128]{3,2,1,0:T(8,128)} %broadcast_in_dim.10), calls=%async_computation.1 | async-start | bytes 2097152 | tf_op jit(solution)/shard_map/all_to_all | solution.py:345
  55.6 119.2 %all-gather.7.cloned.1.call-start = ((), (), s32[]{:S(2)}) async-start(), calls=%async_computation.5 | async-start | bytes 2359296 | tf_op jit(solution)/shard_map/all_gather | solution.py:398
  68.7 62.9 %copy-start.1 = (bf16[4096,128]{1,0:T(8,128)(2,1)S(1)}, bf16[4096,128]{1,0:T(8,128)(2,1)}, u32[]{:S(2)}) copy-start(bf16[4096,128]{1,0:T(8,128)(2,1)} %constant.45.clone.f_ref) | copy-start | bytes 3145732
  143.1 15.2 %all-to-all-start.3 = ((f32[4,64,8,128]{3,2,1,0:T(8,128)}), f32[4,64,8,128]{3,2,1,0:T(8,128)S(1)}, u32[]{:S(2)}, u32[]{:S(2)}) async-start(f32[4,64,8,128]{3,2,1,0:T(8,128)} %broadcast_in_dim.11), calls=%async_computation.3 | async-start | bytes 2097152 | tf_op jit(solution)/shard_map/all_to_all | solution.py:345
  174.8 1.6 copy-start
Sparse Core Ops, SparseCore 0:
  51.1 29.4 all-gather.4
  142.2 28.8 all-gather.6

commit v2 on v1

v2 whole, which is shorter than its diff:
```python
import functools
import math

import jax
import jax.numpy as jnp
import ml_dtypes
import numpy as np
from jax import lax
from jax.experimental import pallas as pl
from jax.experimental.pallas import tpu as pltpu
from jax.sharding import PartitionSpec as P

MX = 8
LANES = 128
WIDE = 256
F32 = jnp.float32
BF16 = jnp.bfloat16
PARAMS = dict(vmem_limit_bytes=50 * 2**20)


def mm(a, b):
    return jnp.dot(a, b, preferred_element_type=F32)


def np_split(table):
    hi = table.astype(ml_dtypes.bfloat16)
    lo = (table - hi.astype(np.float64)).astype(ml_dtypes.bfloat16)
    return hi, lo


def split(x):
    hi = x.astype(BF16).astype(F32)
    return hi, x - hi


def stack_three(x):
    hi, lo = split(x)
    return jnp.concatenate([hi, lo, hi], axis=0).astype(BF16)


def np_three(table):
    hi, lo = np_split(table)
    return np.concatenate([hi, hi, lo], axis=1)


def np_tables(grid, zmodes):
    freqs = np.concatenate([np.arange(MX), grid - MX + np.arange(MX)])
    cells = np.arange(grid)
    ang = 2.0 * math.pi / grid * (freqs[:, None] * cells[None, :] % grid)
    half = 2.0 * math.pi / grid * (freqs[:, None] * (2 * np.arange(grid // 2))[None, :] % grid)
    tw = 2.0 * math.pi / grid * freqs
    count = freqs.size
    fwd_x = np.concatenate([np.cos(ang), -np.sin(ang)], axis=0)
    hi, lo = np_split(fwd_x)
    fwd_x_two = np.concatenate([hi, lo], axis=0)
    fwd_x_three = np_three(fwd_x)
    fwd_y = np_three(np.concatenate([np.cos(half), np.sin(half)], axis=0))
    inv_y = np_three(np.concatenate([np.cos(half.T), np.sin(half.T)], axis=0))
    inv_x = np_three(np.concatenate([np.cos(ang.T), -np.sin(ang.T)], axis=1))
    tw_c = np.ones((count, LANES), np.float32)
    tw_s = np.zeros((count, LANES), np.float32)
    tw_c[:, LANES // 2:] = np.cos(tw)[:, None]
    tw_s[:, LANES // 2:] = np.sin(tw)[:, None]
    kz = np.arange(zmodes)
    zang = 2.0 * math.pi / grid * (cells[:, None] * kz[None, :] % grid)
    scale = np.where(kz == 0, 1.0, 2.0) / float(grid**3)
    waves = np.stack([np.cos(zang), np.sin(zang)], axis=1)
    z_table = np.concatenate([waves, waves * scale], axis=1).astype(np.float32)
    return dict(fwd_x_two=fwd_x_two, fwd_x_three=fwd_x_three, fwd_y=fwd_y, inv_y=inv_y,
                inv_x=inv_x, tw_c=tw_c, tw_s=tw_s, z_table=z_table)


def low_half(shape):
    return lax.broadcasted_iota(jnp.int32, shape, len(shape) - 1) % LANES < LANES // 2


def roll_half(x):
    return pltpu.roll(x, LANES // 2, x.ndim - 1)


def put_rows(g_ref, chunk, first, half):
    for r in range(0, chunk.shape[0], 8):
        for j in range(chunk.shape[1] // LANES):
            g_ref[pl.ds(r * half + first + j, 8, stride=half), :] = chunk[r:r + 8, j * LANES:(j + 1) * LANES]


def get_rows(n_ref, first, blocks, rows, half):
    cols = []
    for j in range(blocks):
        cols.append(jnp.concatenate(
            [n_ref[pl.ds(r * half + first + j, 8, stride=half), :] for r in range(0, rows, 8)], axis=0))
    return jnp.concatenate(cols, axis=1)


def fwd_yz(g_ref, acc_ref, fy, twc, tws, z_ref, kind, z, zmodes, half):
    count = 2 * MX
    low = low_half((count, LANES))
    sign = jnp.where(low, 1.0, -1.0).astype(F32)
    cs = [z_ref[z, kind * zmodes + k] for k in range(zmodes)]
    sn = [z_ref[z, (kind + 1) * zmodes + k] for k in range(zmodes)]
    for a in range(count):
        g = jnp.concatenate([g_ref[a * half:(a + 1) * half, :],
                             g_ref[(count + a) * half:(count + a + 1) * half, :]], axis=1)
        h = mm(fy, stack_three(g))
        re = h[:count, :LANES] + h[count:, LANES:]
        im = h[:count, LANES:] - h[count:, :LANES]
        re2 = re * twc + im * tws
        im2 = im * twc - re * tws
        row = jnp.where(low, re2 + roll_half(re2), im2 + roll_half(im2))
        turned = sign * roll_half(row)
        for k in range(zmodes):
            acc_ref[k, a * count:(a + 1) * count, :] += cs[k] * row + sn[k] * turned


def give_modes(acc_ref, out_ref, zmodes):
    here = out_ref.shape[2]
    for part in range(out_ref.shape[0]):
        out_ref[part] = acc_ref[:, part * here:(part + 1) * here, :]


def inv_zy(m_ref, n_ref, iy, twc, tws, z_ref, kind, z, zmodes, half):
    count = 2 * MX
    low = low_half((count, LANES))
    sign = jnp.where(low, -1.0, 1.0).astype(F32)
    cs = [z_ref[z, kind * zmodes + k] for k in range(zmodes)]
    sn = [z_ref[z, (kind + 1) * zmodes + k] for k in range(zmodes)]
    share = m_ref.shape[2] // count
    for a in range(count):
        owner, rows = a // share, slice(a % share * count, (a % share + 1) * count)
        part = m_ref[owner, 0, rows, :]
        first, second = cs[0] * part, sn[0] * part
        for k in range(1, zmodes):
            part = m_ref[owner, k, rows, :]
            first += cs[k] * part
            second += sn[k] * part
        line = first + sign * roll_half(second)
        other = roll_half(line)
        re = jnp.where(low, line, other)
        im = jnp.where(low, other, line)
        p_re = re * twc - im * tws
        p_im = im * twc + re * tws
        o = mm(iy, stack_three(jnp.concatenate([p_re, p_im], axis=1)))
        n_ref[a * half:(a + 1) * half, :] = o[:half, :LANES] - o[half:, LANES:]
        n_ref[(count + a) * half:(count + a + 1) * half, :] = o[:half, LANES:] + o[half:, :LANES]


def forward_kernel(zmodes, half, z_ref, x_ref, fx_ref, fy_ref, twc_ref, tws_ref, out_ref, acc_ref, g_ref):
    z = pl.program_id(0)

    @pl.when(z == 0)
    def _():
        acc_ref[...] = jnp.zeros_like(acc_ref)

    rows = 4 * MX
    for n in range(0, x_ref.shape[3], WIDE):
        u = mm(fx_ref[...], x_ref[0, 0, :, n:n + WIDE])
        put_rows(g_ref, u[:rows] + u[rows:], n // LANES, half)
    fwd_yz(g_ref, acc_ref, fy_ref[...], twc_ref[...], tws_ref[...], z_ref, 0, z, zmodes, half)

    @pl.when(z == pl.num_programs(0) - 1)
    def _():
        give_modes(acc_ref, out_ref, zmodes)


def middle_kernel(zmodes, half, z_ref, m_ref, x_ref, ct_ref, w_ref, b_ref,
                  iy_ref, ix_ref, fx_ref, fy_ref, twc_ref, tws_ref,
                  out_ref, slope_ref, modes_ref, acc_ref, n_ref, g_ref):
    z = pl.program_id(0)

    @pl.when(z == 0)
    def _():
        acc_ref[...] = jnp.zeros_like(acc_ref)

    twc, tws = twc_ref[...], tws_ref[...]
    inv_zy(m_ref, n_ref, iy_ref[...], twc, tws, z_ref, 2, z, zmodes, half)
    rate = math.sqrt(2.0 / math.pi)
    for n in range(0, x_ref.shape[3], WIDE):
        cols = get_rows(n_ref, n // LANES, WIDE // LANES, 4 * MX, half)
        spectral = mm(ix_ref[...], stack_three(cols))
        u = spectral + mm(x_ref[0, 0, :, n:n + WIDE], w_ref[...]) + b_ref[...]
        square = u * u
        t = jnp.tanh(rate * u * (1.0 + 0.044715 * square))
        gate = 0.5 * (1.0 + t)
        out_ref[0, 0, :, n:n + WIDE] = (u * gate).astype(BF16)
        rise = gate + 0.5 * u * (1.0 - t * t) * (rate * (1.0 + 3.0 * 0.044715 * square))
        slope = ct_ref[0, 0, :, n:n + WIDE].astype(F32) * rise
        slope_ref[0, :, n:n + WIDE] = slope
        put_rows(g_ref, mm(fx_ref[...], stack_three(slope)), n // LANES, half)
    fwd_yz(g_ref, acc_ref, fy_ref[...], twc, tws, z_ref, 2, z, zmodes, half)

    @pl.when(z == pl.num_programs(0) - 1)
    def _():
        give_modes(acc_ref, modes_ref, zmodes)


def final_kernel(zmodes, half, z_ref, m_ref, slope_ref, w_ref, iy_ref, ix_ref, twc_ref, tws_ref,
                 out_ref, n_ref):
    z = pl.program_id(0)
    inv_zy(m_ref, n_ref, iy_ref[...], twc_ref[...], tws_ref[...], z_ref, 0, z, zmodes, half)
    for n in range(0, slope_ref.shape[2], WIDE):
        cols = get_rows(n_ref, n // LANES, WIDE // LANES, 4 * MX, half)
        total = mm(ix_ref[...], stack_three(cols))
        hi, lo = split(slope_ref[0, :, n:n + WIDE])
        total += mm(hi.astype(BF16), w_ref[...]) + mm(lo.astype(BF16), w_ref[...])
        out_ref[0, 0, :, n:n + WIDE] = total.astype(BF16)


def halves(v):
    low = low_half(v.shape)
    other = roll_half(v)
    return jnp.where(low, v, other), jnp.where(low, other, v)


def mix_kernel(spec_ref, w_ref, e_ref, out_ref):
    zmodes, block, _ = spec_ref.shape
    rows = zmodes * block
    both = jnp.concatenate(halves(spec_ref[...].reshape(rows, LANES)), axis=0)
    hi, lo = split(both)
    left = jnp.where(low_half(both.shape), hi, lo).astype(BF16)
    half_re = jnp.zeros((rows, LANES), F32)
    half_im = jnp.zeros((rows, LANES), F32)
    for n in range(0, w_ref.shape[3], WIDE):
        x = mm(left, e_ref[:, n:n + WIDE])
        x_re, x_im = x[:rows], x[rows:]
        w_re = w_ref[0, :, :, n:n + WIDE].astype(F32).reshape(rows, WIDE)
        w_im = w_ref[1, :, :, n:n + WIDE].astype(F32).reshape(rows, WIDE)
        add_re = x_re * w_re - x_im * w_im
        add_im = x_re * w_im + x_im * w_re
        half_re += add_re[:, :LANES] + add_re[:, LANES:]
        half_im += add_im[:, :LANES] + add_im[:, LANES:]
    half_re += roll_half(half_re)
    half_im += roll_half(half_im)
    mixed = jnp.where(low_half(half_re.shape), half_re, half_im).reshape(spec_ref.shape)
    for part in range(out_ref.shape[0]):
        out_ref[part] = mixed


def back_kernel(spec_ref, w_ref, f_ref, out_ref):
    zmodes, block, _ = spec_ref.shape
    rows = zmodes * block
    c_re, c_im = halves(spec_ref[...].reshape(rows, LANES))
    c_re = jnp.concatenate([c_re, c_re], axis=1)
    c_im = jnp.concatenate([c_im, c_im], axis=1)
    total = jnp.zeros((4 * rows, LANES), F32)
    for n in range(0, w_ref.shape[3], WIDE):
        w_re = w_ref[0, :, :, n:n + WIDE].astype(F32).reshape(rows, WIDE)
        w_im = w_ref[1, :, :, n:n + WIDE].astype(F32).reshape(rows, WIDE)
        both = jnp.concatenate([c_re * w_re + c_im * w_im, c_im * w_re - c_re * w_im], axis=0)
        hi, lo = split(both)
        total += mm(jnp.concatenate([hi, lo], axis=0).astype(BF16), f_ref[n:n + WIDE, :])
    total = total[:2 * rows] + total[2 * rows:]
    both = jnp.where(low_half((rows, LANES)), total[:rows], total[rows:]).reshape(spec_ref.shape)
    for part in range(out_ref.shape[0]):
        out_ref[part] = both


def grads_kernel(samples, pairs, v_ref, c_ref, out_ref, x_ref):
    _, zmodes, block, _ = out_ref.shape
    chan = LANES // 2
    low = low_half((block, LANES))
    sign = jnp.where(low_half((samples, LANES)), 1.0, -1.0).astype(F32)
    base = pl.program_id(0) * block
    for k in range(zmodes):
        slot = k % 2
        for q in range(block):
            at = pl.ds(base + (k * pairs + q), samples, stride=zmodes * pairs)
            a = v_ref[at, :]
            b = c_ref[at, :]
            left = jnp.concatenate([a, roll_half(a)], axis=0)
            right = jnp.concatenate([b, sign * roll_half(b)], axis=0)
            l_hi, l_lo = split(left)
            r_hi, r_lo = split(right)
            lhs = jnp.concatenate([l_hi, l_lo, l_hi], axis=0).astype(BF16)[:, :chan]
            rhs = jnp.concatenate([r_hi, r_hi, r_lo], axis=0).astype(BF16)
            x_ref[slot, q * chan:(q + 1) * chan, :] = lax.dot_general(
                lhs, rhs, (((0,), (0,)), ((), ())), preferred_element_type=F32)
        for j in range(chan // 2):
            even = x_ref[slot, pl.ds(2 * j, block, stride=chan), :]
            odd = x_ref[slot, pl.ds(2 * j + 1, block, stride=chan), :]
            lanes = slice(j * LANES, (j + 1) * LANES)
            out_ref[0, k, :, lanes] = jnp.where(low, even, roll_half(odd))
            out_ref[1, k, :, lanes] = jnp.where(low, roll_half(even), odd)


def whole(a):
    rank = a.ndim
    return pl.BlockSpec(a.shape, lambda i: (0,) * rank)


SMEM = pl.BlockSpec(memory_space=pltpu.SMEM)


def on_device(parts, inputs, cotangent, mode_weights, local_weight, local_bias):
    _, planes, grid, width = inputs.shape
    chan = local_weight.shape[0]
    pairs_here, zmodes, entries = mode_weights.shape[1:]
    pairs = pairs_here * parts
    half = grid // 2
    tab = np_tables(grid, zmodes)
    const = {name: jnp.asarray(t) for name, t in tab.items()}
    z_table = lax.dynamic_slice_in_dim(const["z_table"], lax.axis_index("mp") * planes, planes, 0)
    z_table = z_table.reshape(planes, 4 * zmodes)
    weights = jnp.transpose(mode_weights, (0, 2, 1, 3))
    params = pltpu.CompilerParams(**PARAMS)
    plane = pl.BlockSpec((1, 1, grid, width), lambda z: (0, z, 0, 0))
    flat = pl.BlockSpec((1, grid, width), lambda z: (z, 0, 0))
    modes_shape = jax.ShapeDtypeStruct((parts, zmodes, pairs_here, LANES), F32)
    modes_spec = pl.BlockSpec(modes_shape.shape, lambda z: (0, 0, 0, 0))
    acc = pltpu.VMEM((zmodes, pairs, LANES), F32)
    lines = pltpu.VMEM((4 * MX * half, LANES), F32)
    fy, iy, ix, twc, tws = (const[n] for n in ("fwd_y", "inv_y", "inv_x", "tw_c", "tw_s"))
    fx2, fx3 = const["fwd_x_two"], const["fwd_x_three"]

    def exchange(x):
        return lax.all_to_all(x, "mp", 0, 0)

    partial = pl.pallas_call(
        functools.partial(forward_kernel, zmodes, half),
        grid=(planes,),
        in_specs=[SMEM, plane, whole(fx2), whole(fy), whole(twc), whole(tws)],
        out_specs=modes_spec, out_shape=modes_shape, scratch_shapes=[acc, lines],
        compiler_params=params, name="forward",
    )(z_table, inputs, fx2, fy, twc, tws)

    block = 16
    w_spec = pl.BlockSpec((2, zmodes, block, entries), lambda i: (0, 0, i, 0))
    m_spec = pl.BlockSpec((zmodes, block, LANES), lambda i: (0, i, 0))
    many_spec = pl.BlockSpec((parts, zmodes, block, LANES), lambda i: (0, 0, i, 0))
    eye = np.eye(chan, dtype=np.float32)
    expand = np.concatenate([np.repeat(eye, chan, axis=1)] * 2, axis=0)
    fold = np.repeat(np.concatenate([eye, eye], axis=1), chan, axis=0)
    expand, fold = jnp.asarray(expand, BF16), jnp.asarray(fold, BF16)
    spectrum = jnp.sum(exchange(partial), axis=0)
    all_spectra = lax.all_gather(spectrum, "dp")
    mixed = pl.pallas_call(
        mix_kernel,
        grid=(pairs_here // block,),
        in_specs=[m_spec, w_spec, whole(expand)],
        out_specs=many_spec, out_shape=modes_shape,
        compiler_params=params, name="mix",
    )(spectrum, weights, expand)

    repeat = WIDE // chan
    eyes = jnp.eye(repeat, dtype=BF16)
    w_wide = jnp.kron(eyes, local_weight)
    wt_wide = jnp.kron(eyes, local_weight.T)
    bias = jnp.tile(local_bias, repeat)[None, :]
    outputs, slope, cot_partial = pl.pallas_call(
        functools.partial(middle_kernel, zmodes, half),
        grid=(planes,),
        in_specs=[SMEM, modes_spec, plane, plane, whole(w_wide), whole(bias), whole(iy), whole(ix),
                               whole(fx3), whole(fy), whole(twc), whole(tws)],
        out_specs=[plane, flat, modes_spec],
        out_shape=[jax.ShapeDtypeStruct(inputs.shape, BF16),
                   jax.ShapeDtypeStruct((planes, grid, width), F32), modes_shape],
        scratch_shapes=[acc, lines, lines],
        compiler_params=params, name="middle",
    )(z_table, exchange(mixed), inputs, cotangent, w_wide, bias, iy, ix, fx3, fy, twc, tws)

    cot_spectrum = jnp.sum(exchange(cot_partial), axis=0)
    all_cots = lax.all_gather(cot_spectrum, "dp")
    back = pl.pallas_call(
        back_kernel,
        grid=(pairs_here // block,),
        in_specs=[m_spec, w_spec, whole(fold)],
        out_specs=many_spec, out_shape=modes_shape,
        compiler_params=params, name="back",
    )(cot_spectrum, weights, fold)
    back_lines = exchange(back)

    samples = all_spectra.shape[0]
    rows = samples * zmodes * pairs_here
    gathered = pl.BlockSpec((rows, LANES), lambda i: (0, 0))
    group = 8
    mode_grads = pl.pallas_call(
        functools.partial(grads_kernel, samples, pairs_here),
        grid=(pairs_here // group,),
        in_specs=[gathered, gathered],
        out_specs=pl.BlockSpec((2, zmodes, group, entries), lambda i: (0, 0, i, 0)),
        out_shape=jax.ShapeDtypeStruct((2, zmodes, pairs_here, entries), F32),
        scratch_shapes=[pltpu.VMEM((2, group * chan, LANES), F32)],
        cost_estimate=pl.CostEstimate(flops=2 * 2**30, bytes_accessed=2**26, transcendentals=0),
        compiler_params=params, name="grads",
    )(all_spectra.reshape(rows, LANES), all_cots.reshape(rows, LANES))
    mode_grads, slope = lax.optimization_barrier((mode_grads, slope))
    mode_grads = jnp.transpose(mode_grads, (0, 2, 1, 3))

    input_grads = pl.pallas_call(
        functools.partial(final_kernel, zmodes, half),
        grid=(planes,),
        in_specs=[SMEM, modes_spec, flat, whole(wt_wide), whole(iy), whole(ix), whole(twc), whole(tws)],
        out_specs=plane, out_shape=jax.ShapeDtypeStruct(inputs.shape, BF16),
        scratch_shapes=[lines],
        compiler_params=params, name="final",
    )(z_table, back_lines, slope, wt_wide, iy, ix, twc, tws)
    return (outputs, input_grads, mode_grads)


def solution(mesh):
    field = P("dp", "mp", None, None)
    weights = P(None, "mp", None, None)
    return jax.shard_map(
        functools.partial(on_device, mesh.shape["mp"]),
        mesh=mesh,
        in_specs=(field, field, weights, P(), P()),
        out_specs=(field, field, weights),
        check_vma=False,
    )
```

time: 230 us -> 206 us (0.90)
  local copies, waits for them, and re-layouts: 37.5 us -> 9.22 us
  blocking collectives: 16.1 us -> 32.5 us
  starting transfers between devices: 12.4 us -> 7.09 us
  Pallas kernels: 120 us -> 115 us
    unnamed x32 -> x36, local copies, waits for them, and re-layouts: 34.8 us -> 7.72 us
    all_to_all x3 -> x2, waiting for transfers between devices: 26.6 us -> 10.1 us  [exchange(): return lax.all_to_all(x, 'mp', 0, 0)]
    all_to_all x1 -> x2, blocking collectives: 16.1 us -> 32.5 us  [exchange(): return lax.all_to_all(x, 'mp', 0, 0)]
    all_gather x1, waiting for transfers between devices: 0.01 us -> 14.4 us  [on_device(): all_cots = lax.all_gather(cot_spectrum, 'dp')]
    all_to_all x3 -> x2, starting transfers between devices: 12.4 us -> 7.01 us  [exchange(): return lax.all_to_all(x, 'mp', 0, 0)]
    pallas_call x3, Pallas kernels: 45 us -> 41.5 us  [the longest x1 26.1 us: on_device(): pl.pallas_call(functools.partial(grads_kernel, samples, pairs_here), grid...]
  transfers between devices with their start and end apart: 5 -> 4, of which waited for: 3 -> 2; matrix products, arithmetic and copies ran while one was open for 6% -> 1% of each run, Pallas kernels for 32% -> 43%
where the time goes in v2:
time: 206 us; the launch traced here: 204 us
  Pallas kernels  115 us (56%)
  blocking collectives  32.5 us (16%)
  waiting for transfers between devices  24.6 us (12%)
  between operations  14.2 us (7%)
  local copies, waits for them, and re-layouts  9.22 us (4%)
  starting transfers between devices  7.09 us (3%)
    pallas_call x1, Pallas kernels, on_device(): pl.pallas_call(functools.partial(middle_kernel, zmodes, half), grid=(plan...  46.3 us
    all_to_all x2, blocking collectives, exchange(): return lax.all_to_all(x, 'mp', 0, 0)  32.5 us
    pallas_call x1, Pallas kernels, on_device(): pl.pallas_call(functools.partial(grads_kernel, samples, pairs_here), grid...  26.1 us
    pallas_call x1, Pallas kernels, on_device(): pl.pallas_call(functools.partial(final_kernel, zmodes, half), grid=(plane...  16.1 us
    all_gather x1, waiting for transfers between devices, on_device(): all_cots = lax.all_gather(cot_spectrum, 'dp')  14.4 us
    pallas_call x1, Pallas kernels, on_device(): pl.pallas_call(functools.partial(forward_kernel, zmodes, half), grid=(pla...  11 us
    all_to_all x2, waiting for transfers between devices, exchange(): return lax.all_to_all(x, 'mp', 0, 0)  10.1 us
    unnamed x36, local copies, waits for them, and re-layouts  7.72 us
  transfers between devices with their start and end apart: 4, of which 2 were waited for; matrix products, arithmetic and copies ran while one was open for 1% of the time, Pallas kernels for 43%

profile of v2, /device:TPU:0, one launch (start us, length us, event | category | flops | bytes accessed | tf_op | source)
XLA Modules:
  0.0 204.3 jit_solution(6652168591606289624)
XLA Ops:
  7.2 0.0 all-gather.5.cloned.1.call-start
  7.2 0.8 constant_dynamic-slice_fusion
  8.0 0.1 copy.24.z_ref
  8.1 0.0 copy-start.6
  8.1 0.7 copy-done.6
  8.8 0.0 copy-start.8
  8.8 0.7 copy-done.8
  9.5 0.0 copy-start.12
  9.5 0.7 copy-done.12
  10.2 0.0 copy-start.15
  10.2 0.7 copy-done.15
  10.9 0.0 copy-start.5
  10.9 11.0 %forward.1 = f32[4,7,64,128]{3,2,1,0:T(8,128)S(1)} custom-call(f32[12,28]{1,0:T(8,128)S(1)} %copy.24.z_ref, bf16[1,12,48,3072]{3,2,1,0:T(8,128)(2,1)} %x_ref.3, bf16[64,48]{1,0:T(8,128)(2,1)S(1)} %copy-done.15, bf16[32,72]{1,0:T(8,128)(2,1)S(1)} %copy-done.12, f32[16,128]{1,0:T(8,128)S(1)} %copy-done.6, f32[16,128]{1,0:T(8,128)S(1)} %copy-done.8), custom_call_target="tpu_custom_call" | custom-call | tf_op jit(solution)/shard_map/forward/pallas_call | solution.py:317
  21.9 17.7 %all_to_all.20 = f32[4,7,64,128]{3,2,1,0:T(8,128)S(1)} all-to-all(f32[4,7,64,128]{3,2,1,0:T(8,128)S(1)} %forward.1), channel_id=1, replica_groups=mesh['dp'=8,'mp'=4] {'mp'}, dimensions={0} | all-to-all | bytes 1835008 | tf_op jit(solution)/shard_map/all_to_all | solution.py:315
  39.6 0.7 reduce_sum.18.spec_ref
  40.4 0.0 all-gather.5.cloned.1.call-update
  40.4 0.0 copy-done.5
  40.4 0.0 copy-start
  40.4 0.9 copy-done
  41.4 0.0 copy-start.16
  41.4 0.0 copy-start.17
  41.4 0.0 copy-start.7
  41.4 0.0 copy-start.9
  41.4 0.0 copy-start.10
  41.4 0.0 copy-start.11
  41.4 0.0 copy-start.13
  41.4 0.0 copy-start.14
  41.4 7.7 %mix.1 = f32[4,7,64,128]{3,2,1,0:T(8,128)} custom-call(f32[7,64,128]{2,1,0:T(8,128)S(1)} %copy-done, bf16[2,7,64,4096]{3,2,1,0:T(8,128)(2,1)} %bitcast.9, bf16[128,4096]{1,0:T(8,128)(2,1)S(1)} %copy-done.5), custom_call_target="tpu_custom_call" | custom-call | tf_op jit(solution)/shard_map/mix/pallas_call | solution.py:335
  49.1 3.5 %all-to-all-start.1 = ((f32[4,7,64,128]{3,2,1,0:T(8,128)}), f32[4,7,64,128]{3,2,1,0:T(8,128)S(1)}, u32[]{:S(2)}, u32[]{:S(2)}) async-start(f32[4,7,64,128]{3,2,1,0:T(8,128)} %mix.1), calls=%async_computation.1 | async-start | bytes 1835008 | tf_op jit(solution)/shard_map/all_to_all | solution.py:315
  52.6 0.0 all-gather.7.cloned.1.call-start
  52.7 0.0 copy-done.16
  52.7 0.1 copy.25
  52.8 0.3 broadcast_multiply_fusion
  53.1 0.2 mul.48.w_ref
  53.3 0.0 copy-done.17
  53.3 0.1 broadcast_in_dim_tile.3.b_ref
  53.4 10.1 %all-to-all-done.1.m_ref = f32[4,7,64,128]{3,2,1,0:T(8,128)S(1)} async-done(((f32[4,7,64,128]{3,2,1,0:T(8,128)}), f32[4,7,64,128]{3,2,1,0:T(8,128)S(1)}, u32[]{:S(2)}, u32[]{:S(2)}) %all-to-all-start.1) | async-done | bytes 917536 | tf_op jit(solution)/shard_map/all_to_all | solution.py:315
  63.5 0.0 copy-done.7
  63.5 0.0 copy-done.9
  63.5 0.0 copy-done.10
  63.5 0.0 copy-done.11
  63.5 0.0 copy-done.13
  63.6 0.0 copy-done.14
  63.6 46.3 %middle.1 = (bf16[1,12,48,3072]{3,2,1,0:T(8,128)(2,1)}, f32[12,48,3072]{2,1,0:T(8,128)}, f32[4,7,64,128]{3,2,1,0:T(8,128)S(1)}) custom-call(f32[12,28]{1,0:T(8,128)S(1)} %copy.24.z_ref, f32[4,7,64,128]{3,2,1,0:T(8,128)S(1)} %all-to-all-done.1.m_ref, bf16[1,12,48,3072]{3,2,1,0:T(8,128)(2,1)} %x_ref.3, bf16[1,12,48,3072]{3,2,1,0:T(8,128)(2,1)} %ct_ref.1, ...), custom_call_target="tpu_custom_call" | custom-call | tf_op jit(solution)/shard_map/middle/pallas_call | solution.py:348
  109.9 0.0 copy-start.4
  109.9 14.8 %all_to_all.21 = f32[4,7,64,128]{3,2,1,0:T(8,128)S(1)} all-to-all(f32[4,7,64,128]{3,2,1,0:T(8,128)S(1)} %get-tuple-element.9), channel_id=1, replica_groups=mesh['dp'=8,'mp'=4] {'mp'}, dimensions={0} | all-to-all | bytes 1835008 | tf_op jit(solution)/shard_map/all_to_all | solution.py:315
  124.7 0.8 reduce_sum.19.spec_ref
  125.5 0.0 all-gather.7.cloned.1.call-update
  125.5 0.0 copy-done.4
  125.5 0.0 copy-start.1
  125.5 0.9 copy-done.1
  126.5 7.7 %back.1 = f32[4,7,64,128]{3,2,1,0:T(8,128)} custom-call(f32[7,64,128]{2,1,0:T(8,128)S(1)} %copy-done.1, bf16[2,7,64,4096]{3,2,1,0:T(8,128)(2,1)} %bitcast.10, bf16[4096,128]{1,0:T(8,128)(2,1)S(1)} %copy-done.4), custom_call_target="tpu_custom_call" | custom-call | tf_op jit(solution)/shard_map/back/pallas_call | solution.py:362
  134.2 3.5 %all-to-all-start.3 = ((f32[4,7,64,128]{3,2,1,0:T(8,128)}), f32[4,7,64,128]{3,2,1,0:T(8,128)S(1)}, u32[]{:S(2)}, u32[]{:S(2)}) async-start(f32[4,7,64,128]{3,2,1,0:T(8,128)} %back.1), calls=%async_computation.3 | async-start | bytes 1835008 | tf_op jit(solution)/shard_map/all_to_all | solution.py:315
  137.7 0.2 mul.51.w_ref
  137.9 0.0 all-gather.5.cloned.1.call-done
  137.9 14.4 %all-gather.7.cloned.1.call-done = f32[56,64,128]{2,1,0:T(8,128)} async-done(((f32[7,64,128]{2,1,0:T(8,128)}), f32[56,64,128]{2,1,0:T(8,128)}) %all-gather.7.cloned.1.call-update) | async-done | bytes 1835024 | tf_op jit(solution)/shard_map/all_gather | solution.py:361
  152.3 0.0 copy-start.2
  152.3 1.5 copy-done.2
  153.8 0.0 copy-start.3
  153.8 1.5 copy-done.3
  155.3 26.1 %grads.1 = f32[2,7,64,4096]{3,2,1,0:T(8,128)} custom-call(f32[3584,128]{1,0:T(8,128)S(1)} %bitcast.7, f32[3584,128]{1,0:T(8,128)S(1)} %bitcast.8), custom_call_target="tpu_custom_call" | custom-call | flops 2147483648 | bytes 67108864 | tf_op jit(solution)/shard_map/grads/pallas_call | solution.py:375
  181.4 0.0 all-to-all-done.3.m_ref
  181.4 16.1 %final.1 = bf16[1,12,48,3072]{3,2,1,0:T(8,128)(2,1)} custom-call(f32[12,28]{1,0:T(8,128)S(1)} %copy.24.z_ref, f32[4,7,64,128]{3,2,1,0:T(8,128)S(1)} %all-to-all-done.3.m_ref, f32[12,48,3072]{2,1,0:T(8,128)} %get-tuple-element.11.slope_ref, bf16[256,256]{1,0:T(8,128)(2,1)S(1)} %mul.51.w_ref, bf16[48,48]{1,0:T(8,128)(2,1)S(1)} %copy-done.10, ...), custom_call_target="tpu_custom_call" | custom-call | tf_op jit(solution)/shard_map/final/pallas_call | solution.py:388
  (3 shorter events, 0.0 us)
Async XLA Ops:
  7.2 130.7 %all-gather.5.cloned.1.call-start = ((), (), s32[]{:S(2)}) async-start(), calls=%async_computation.4 | async-start | bytes 2064384 | tf_op jit(solution)/shard_map/all_gather | solution.py:334
  8.1 0.7 copy-start.6
  8.8 0.7 copy-start.8
  9.5 0.7 copy-start.12
  10.2 0.7 copy-start.15
  10.9 29.5 %copy-start.5 = (bf16[128,4096]{1,0:T(8,128)(2,1)S(1)}, bf16[128,4096]{1,0:T(8,128)(2,1)}, u32[]{:S(2)}) copy-start(bf16[128,4096]{1,0:T(8,128)(2,1)} %constant.40.clone.e_ref) | copy-start | bytes 3145732
  40.4 0.9 copy-start
  41.4 11.3 %copy-start.16 = (bf16[64,64]{1,0:T(8,128)(2,1)S(1)}, bf16[64,64]{1,0:T(8,128)(2,1)}, u32[]{:S(2)}) copy-start(bf16[64,64]{1,0:T(8,128)(2,1)} %param.18) | copy-start | bytes 24580
  41.4 11.9 %copy-start.17 = (f32[64]{0:T(128)S(1)}, f32[64]{0:T(128)}, u32[]{:S(2)}) copy-start(f32[64]{0:T(128)} %param.19) | copy-start | bytes 772
  41.4 22.2 %copy-start.7 = (f32[16,128]{1,0:T(8,128)S(1)}, f32[16,128]{1,0:T(8,128)}, u32[]{:S(2)}) copy-start(f32[16,128]{1,0:T(8,128)} %constant.37.clone.twc_ref) | copy-start | bytes 24580
  41.4 22.2 %copy-start.9 = (f32[16,128]{1,0:T(8,128)S(1)}, f32[16,128]{1,0:T(8,128)}, u32[]{:S(2)}) copy-start(f32[16,128]{1,0:T(8,128)} %constant.38.clone.tws_ref) | copy-start | bytes 24580
  41.4 22.2 %copy-start.10 = (bf16[48,48]{1,0:T(8,128)(2,1)S(1)}, bf16[48,48]{1,0:T(8,128)(2,1)}, u32[]{:S(2)}) copy-start(bf16[48,48]{1,0:T(8,128)(2,1)} %constant.35.clone.iy_ref) | copy-start | bytes 13828
  41.4 22.2 %copy-start.11 = (bf16[48,96]{1,0:T(8,128)(2,1)S(1)}, bf16[48,96]{1,0:T(8,128)(2,1)}, u32[]{:S(2)}) copy-start(bf16[48,96]{1,0:T(8,128)(2,1)} %constant.36.clone.ix_ref) | copy-start | bytes 27652
  41.4 22.2 %copy-start.13 = (bf16[32,72]{1,0:T(8,128)(2,1)S(1)}, bf16[32,72]{1,0:T(8,128)(2,1)}, u32[]{:S(2)}) copy-start(bf16[32,72]{1,0:T(8,128)(2,1)} %constant.34.clone.fy_ref) | copy-start | bytes 13828
  41.4 22.1 %copy-start.14 = (bf16[32,144]{1,0:T(8,128)(2,1)S(1)}, bf16[32,144]{1,0:T(8,128)(2,1)}, u32[]{:S(2)}) copy-start(bf16[32,144]{1,0:T(8,128)(2,1)} %constant.33.clone.fx_ref) | copy-start | bytes 27652
  49.1 14.4 %all-to-all-start.1 = ((f32[4,7,64,128]{3,2,1,0:T(8,128)}), f32[4,7,64,128]{3,2,1,0:T(8,128)S(1)}, u32[]{:S(2)}, u32[]{:S(2)}) async-start(f32[4,7,64,128]{3,2,1,0:T(8,128)} %mix.1), calls=%async_computation.1 | async-start | bytes 1835008 | tf_op jit(solution)/shard_map/all_to_all | solution.py:315
  52.6 99.7 %all-gather.7.cloned.1.call-start = ((), (), s32[]{:S(2)}) async-start(), calls=%async_computation.5 | async-start | bytes 2064384 | tf_op jit(solution)/shard_map/all_gather | solution.py:361
  109.9 15.6 %copy-start.4 = (bf16[4096,128]{1,0:T(8,128)(2,1)S(1)}, bf16[4096,128]{1,0:T(8,128)(2,1)}, u32[]{:S(2)}) copy-start(bf16[4096,128]{1,0:T(8,128)(2,1)} %constant.41.clone.f_ref) | copy-start | bytes 3145732
  125.5 0.9 copy-start.1
  134.2 47.2 %all-to-all-start.3 = ((f32[4,7,64,128]{3,2,1,0:T(8,128)}), f32[4,7,64,128]{3,2,1,0:T(8,128)S(1)}, u32[]{:S(2)}, u32[]{:S(2)}) async-start(f32[4,7,64,128]{3,2,1,0:T(8,128)} %back.1), calls=%async_computation.3 | async-start | bytes 1835008 | tf_op jit(solution)/shard_map/all_to_all | solution.py:315
  152.3 1.5 copy-start.2
  153.8 1.5 copy-start.3
Sparse Core Ops, SparseCore 0:
  40.5 26.6 all-gather.4
  125.6 26.6 all-gather.6

commit v3 on v2

--- a/solution.py
+++ b/solution.py
@@ -164,7 +164,7 @@
 
 def middle_kernel(zmodes, half, z_ref, m_ref, x_ref, ct_ref, w_ref, b_ref,
                   iy_ref, ix_ref, fx_ref, fy_ref, twc_ref, tws_ref,
-                  out_ref, slope_ref, modes_ref, acc_ref, n_ref, g_ref):
+                  out_ref, slope_ref, modes_ref, acc_ref, n_ref, g_ref, loc_ref):
     z = pl.program_id(0)
 
     @pl.when(z == 0)
@@ -174,10 +174,13 @@
     twc, tws = twc_ref[...], tws_ref[...]
     inv_zy(m_ref, n_ref, iy_ref[...], twc, tws, z_ref, 2, z, zmodes, half)
     rate = math.sqrt(2.0 / math.pi)
+    width, tall = x_ref.shape[3], x_ref.shape[2]
+    loc_ref[...] = mm(jnp.concatenate([x_ref[0, 0, :, n:n + WIDE] for n in range(0, width, WIDE)], axis=0), w_ref[...])
     for n in range(0, x_ref.shape[3], WIDE):
         cols = get_rows(n_ref, n // LANES, WIDE // LANES, 4 * MX, half)
         spectral = mm(ix_ref[...], stack_three(cols))
-        u = spectral + mm(x_ref[0, 0, :, n:n + WIDE], w_ref[...]) + b_ref[...]
+        at = n // WIDE * tall
+        u = spectral + loc_ref[at:at + tall, :] + b_ref[...]
         square = u * u
         t = jnp.tanh(rate * u * (1.0 + 0.044715 * square))
         gate = 0.5 * (1.0 + t)
@@ -194,14 +197,19 @@
 
 
 def final_kernel(zmodes, half, z_ref, m_ref, slope_ref, w_ref, iy_ref, ix_ref, twc_ref, tws_ref,
-                 out_ref, n_ref):
+                 out_ref, n_ref, loc_ref):
     z = pl.program_id(0)
     inv_zy(m_ref, n_ref, iy_ref[...], twc_ref[...], tws_ref[...], z_ref, 0, z, zmodes, half)
-    for n in range(0, slope_ref.shape[2], WIDE):
+    width, tall = slope_ref.shape[2], slope_ref.shape[1]
+    pieces = [split(slope_ref[0, :, n:n + WIDE]) for n in range(0, width, WIDE)]
+    pieces = [piece[part].astype(BF16) for part in range(2) for piece in pieces]
+    loc_ref[...] = mm(jnp.concatenate(pieces, axis=0), w_ref[...])
+    below = width // WIDE * tall
+    for n in range(0, width, WIDE):
         cols = get_rows(n_ref, n // LANES, WIDE // LANES, 4 * MX, half)
         total = mm(ix_ref[...], stack_three(cols))
-        hi, lo = split(slope_ref[0, :, n:n + WIDE])
-        total += mm(hi.astype(BF16), w_ref[...]) + mm(lo.astype(BF16), w_ref[...])
+        at = n // WIDE * tall
+        total += loc_ref[at:at + tall, :] + loc_ref[below + at:below + at + tall, :]
         out_ref[0, 0, :, n:n + WIDE] = total.astype(BF16)
 
 
@@ -353,7 +361,7 @@
         out_specs=[plane, flat, modes_spec],
         out_shape=[jax.ShapeDtypeStruct(inputs.shape, BF16),
                    jax.ShapeDtypeStruct((planes, grid, width), F32), modes_shape],
-        scratch_shapes=[acc, lines, lines],
+        scratch_shapes=[acc, lines, lines, pltpu.VMEM((width // WIDE * grid, WIDE), F32)],
         compiler_params=params, name="middle",
     )(z_table, exchange(mixed), inputs, cotangent, w_wide, bias, iy, ix, fx3, fy, twc, tws)
 
@@ -368,6 +376,16 @@
     )(cot_spectrum, weights, fold)
     back_lines = exchange(back)
 
+    input_grads = pl.pallas_call(
+        functools.partial(final_kernel, zmodes, half),
+        grid=(planes,),
+        in_specs=[SMEM, modes_spec, flat, whole(wt_wide), whole(iy), whole(ix), whole(twc), whole(tws)],
+        out_specs=plane, out_shape=jax.ShapeDtypeStruct(inputs.shape, BF16),
+        scratch_shapes=[lines, pltpu.VMEM((2 * (width // WIDE) * grid, WIDE), F32)],
+        compiler_params=params, name="final",
+    )(z_table, back_lines, slope, wt_wide, iy, ix, twc, tws)
+
+    all_cots, input_grads = lax.optimization_barrier((all_cots, input_grads))
     samples = all_spectra.shape[0]
     rows = samples * zmodes * pairs_here
     gathered = pl.BlockSpec((rows, LANES), lambda i: (0, 0))
@@ -382,17 +400,7 @@
         cost_estimate=pl.CostEstimate(flops=2 * 2**30, bytes_accessed=2**26, transcendentals=0),
         compiler_params=params, name="grads",
     )(all_spectra.reshape(rows, LANES), all_cots.reshape(rows, LANES))
-    mode_grads, slope = lax.optimization_barrier((mode_grads, slope))
     mode_grads = jnp.transpose(mode_grads, (0, 2, 1, 3))
-
-    input_grads = pl.pallas_call(
-        functools.partial(final_kernel, zmodes, half),
-        grid=(planes,),
-        in_specs=[SMEM, modes_spec, flat, whole(wt_wide), whole(iy), whole(ix), whole(twc), whole(tws)],
-        out_specs=plane, out_shape=jax.ShapeDtypeStruct(inputs.shape, BF16),
-        scratch_shapes=[lines],
-        compiler_params=params, name="final",
-    )(z_table, back_lines, slope, wt_wide, iy, ix, twc, tws)
     return (outputs, input_grads, mode_grads)
 
 

time: 206 us -> 194 us (0.942)
  Pallas kernels: 115 us -> 90.3 us
  waiting for transfers between devices: 24.6 us -> 39.1 us
    pallas_call x1, Pallas kernels: 46.3 us -> 24.1 us  [on_device(): pl.pallas_call(functools.partial(middle_kernel, zmodes, half), grid=(plan...]
    all_gather x1, waiting for transfers between devices: 0.02 us -> 18.2 us  [on_device(): all_spectra = lax.all_gather(spectrum, 'dp')]
    all_gather x1, waiting for transfers between devices: 14.4 us -> 0.01 us  [on_device(): all_cots = lax.all_gather(cot_spectrum, 'dp')]
    all_to_all x2, waiting for transfers between devices: 10.1 us -> 20.2 us  [exchange(): return lax.all_to_all(x, 'mp', 0, 0)]
    pallas_call x1, Pallas kernels: 16.1 us -> 13.6 us  [on_device(): pl.pallas_call(functools.partial(final_kernel, zmodes, half), grid=(plane...]
  transfers between devices with their start and end apart: 4 -> 4, of which waited for: 2 -> 3; matrix products, arithmetic and copies ran while one was open for 1% -> 0% of each run, Pallas kernels for 43% -> 11%
where the time goes in v3:
time: 194 us; the launch traced here: 192 us
  Pallas kernels  90.3 us (47%)
  waiting for transfers between devices  39.1 us (20%)
  blocking collectives  32.4 us (17%)
  between operations  14.2 us (7%)
  local copies, waits for them, and re-layouts  8.3 us (4%)
  starting transfers between devices  7.1 us (4%)
    all_to_all x2, blocking collectives, exchange(): return lax.all_to_all(x, 'mp', 0, 0)  32.4 us
    pallas_call x1, Pallas kernels, on_device(): pl.pallas_call(functools.partial(grads_kernel, samples, pairs_here), grid...  26.1 us
    pallas_call x1, Pallas kernels, on_device(): pl.pallas_call(functools.partial(middle_kernel, zmodes, half), grid=(plan...  24.1 us
    all_to_all x2, waiting for transfers between devices, exchange(): return lax.all_to_all(x, 'mp', 0, 0)  20.2 us
    all_gather x1, waiting for transfers between devices, on_device(): all_spectra = lax.all_gather(spectrum, 'dp')  18.2 us
    pallas_call x1, Pallas kernels, on_device(): pl.pallas_call(functools.partial(final_kernel, zmodes, half), grid=(plane...  13.6 us
    pallas_call x1, Pallas kernels, on_device(): pl.pallas_call(functools.partial(forward_kernel, zmodes, half), grid=(pla...  11 us
    pallas_call x1, Pallas kernels, on_device(): pl.pallas_call(back_kernel, grid=(pairs_here // block,), in_specs=[m_spec...  7.71 us
  transfers between devices with their start and end apart: 4, of which 3 were waited for; matrix products, arithmetic and copies ran while one was open for 0% of the time, Pallas kernels for 11%

profile of v3, /device:TPU:0, one launch (start us, length us, event | category | flops | bytes accessed | tf_op | source)
XLA Modules:
  0.0 192.5 jit_solution(12955733705430415581)
XLA Ops:
  7.2 0.8 constant_dynamic-slice_fusion
  8.0 0.1 copy.24.z_ref
  8.1 0.0 copy-start.6
  8.1 0.7 copy-done.6
  8.8 0.0 copy-start.8
  8.8 0.7 copy-done.8
  9.5 0.0 copy-start.12
  9.5 0.7 copy-done.12
  10.2 0.0 copy-start.15
  10.2 0.7 copy-done.15
  10.9 0.0 copy-start.5
  10.9 11.0 %forward.1 = f32[4,7,64,128]{3,2,1,0:T(8,128)S(1)} custom-call(f32[12,28]{1,0:T(8,128)S(1)} %copy.24.z_ref, bf16[1,12,48,3072]{3,2,1,0:T(8,128)(2,1)} %x_ref.3, bf16[64,48]{1,0:T(8,128)(2,1)S(1)} %copy-done.15, bf16[32,72]{1,0:T(8,128)(2,1)S(1)} %copy-done.12, f32[16,128]{1,0:T(8,128)S(1)} %copy-done.8, f32[16,128]{1,0:T(8,128)S(1)} %copy-done.6), custom_call_target="tpu_custom_call" | custom-call | tf_op jit(solution)/shard_map/forward/pallas_call | solution.py:325
  21.9 17.7 %all_to_all.20 = f32[4,7,64,128]{3,2,1,0:T(8,128)S(1)} all-to-all(f32[4,7,64,128]{3,2,1,0:T(8,128)S(1)} %forward.1), channel_id=1, replica_groups=mesh['dp'=8,'mp'=4] {'mp'}, dimensions={0} | all-to-all | bytes 1835008 | tf_op jit(solution)/shard_map/all_to_all | solution.py:323
  39.6 0.1 reduce_sum.18.spec_ref
  39.6 0.0 copy-start
  39.7 0.0 copy-done.5
  39.7 0.0 copy-start.17
  39.7 0.0 copy-start.16
  39.7 0.0 copy-start.7
  39.7 0.0 copy-start.9
  39.7 0.0 copy-start.10
  39.7 0.0 copy-start.11
  39.7 0.0 copy-start.13
  39.8 0.0 copy-start.14
  39.8 7.7 %mix.1 = f32[4,7,64,128]{3,2,1,0:T(8,128)} custom-call(f32[7,64,128]{2,1,0:T(8,128)S(1)} %reduce_sum.18.spec_ref, bf16[2,7,64,4096]{3,2,1,0:T(8,128)(2,1)} %bitcast.10, bf16[128,4096]{1,0:T(8,128)(2,1)S(1)} %copy-done.5), custom_call_target="tpu_custom_call" | custom-call | tf_op jit(solution)/shard_map/mix/pallas_call | solution.py:343
  47.5 0.0 copy-done
  47.5 3.5 %all-to-all-start.1 = ((f32[4,7,64,128]{3,2,1,0:T(8,128)}), f32[4,7,64,128]{3,2,1,0:T(8,128)S(1)}, u32[]{:S(2)}, u32[]{:S(2)}) async-start(f32[4,7,64,128]{3,2,1,0:T(8,128)} %mix.1), calls=%async_computation.1 | async-start | bytes 1835008 | tf_op jit(solution)/shard_map/all_to_all | solution.py:323
  51.0 0.0 all-gather.5.cloned.1.call-start
  51.0 0.0 copy-done.17
  51.1 0.1 broadcast_in_dim_tile.3.b_ref
  51.1 0.0 copy-done.16
  51.1 0.1 copy.25
  51.2 0.3 broadcast_multiply_fusion
  51.5 0.2 mul.48.w_ref
  51.7 10.2 %all-to-all-done.1.m_ref = f32[4,7,64,128]{3,2,1,0:T(8,128)S(1)} async-done(((f32[4,7,64,128]{3,2,1,0:T(8,128)}), f32[4,7,64,128]{3,2,1,0:T(8,128)S(1)}, u32[]{:S(2)}, u32[]{:S(2)}) %all-to-all-start.1) | async-done | bytes 917536 | tf_op jit(solution)/shard_map/all_to_all | solution.py:323
  61.9 0.0 copy-done.7
  61.9 0.0 copy-done.9
  61.9 0.0 copy-done.10
  61.9 0.0 copy-done.11
  61.9 0.0 copy-done.13
  62.0 0.0 copy-done.14
  62.0 24.1 %middle.1 = (bf16[1,12,48,3072]{3,2,1,0:T(8,128)(2,1)}, f32[12,48,3072]{2,1,0:T(8,128)}, f32[4,7,64,128]{3,2,1,0:T(8,128)S(1)}) custom-call(f32[12,28]{1,0:T(8,128)S(1)} %copy.24.z_ref, f32[4,7,64,128]{3,2,1,0:T(8,128)S(1)} %all-to-all-done.1.m_ref, bf16[1,12,48,3072]{3,2,1,0:T(8,128)(2,1)} %x_ref.3, bf16[1,12,48,3072]{3,2,1,0:T(8,128)(2,1)} %ct_ref.1, ...), custom_call_target="tpu_custom_call" | custom-call | tf_op jit(solution)/shard_map/middle/pallas_call | solution.py:356
  86.1 0.0 copy-start.4
  86.1 14.7 %all_to_all.21 = f32[4,7,64,128]{3,2,1,0:T(8,128)S(1)} all-to-all(f32[4,7,64,128]{3,2,1,0:T(8,128)S(1)} %get-tuple-element.9), channel_id=1, replica_groups=mesh['dp'=8,'mp'=4] {'mp'}, dimensions={0} | all-to-all | bytes 1835008 | tf_op jit(solution)/shard_map/all_to_all | solution.py:323
  100.8 0.7 reduce_sum.19.spec_ref
  101.6 0.0 all-gather.5.cloned.1.call-update
  101.6 0.0 all-gather.7.cloned.1.call-start
  101.6 0.7 all-gather.7.cloned.1.call-update
  102.3 0.0 copy-done.4
  102.4 0.0 copy-start.1
  102.4 0.9 copy-done.1
  103.3 7.7 %back.1 = f32[4,7,64,128]{3,2,1,0:T(8,128)} custom-call(f32[7,64,128]{2,1,0:T(8,128)S(1)} %copy-done.1, bf16[2,7,64,4096]{3,2,1,0:T(8,128)(2,1)} %bitcast.11, bf16[4096,128]{1,0:T(8,128)(2,1)S(1)} %copy-done.4), custom_call_target="tpu_custom_call" | custom-call | tf_op jit(solution)/shard_map/back/pallas_call | solution.py:370
  111.0 3.5 %all-to-all-start.3 = ((f32[4,7,64,128]{3,2,1,0:T(8,128)}), f32[4,7,64,128]{3,2,1,0:T(8,128)S(1)}, u32[]{:S(2)}, u32[]{:S(2)}) async-start(f32[4,7,64,128]{3,2,1,0:T(8,128)} %back.1), calls=%async_computation.3 | async-start | bytes 1835008 | tf_op jit(solution)/shard_map/all_to_all | solution.py:323
  114.5 0.2 mul.51.w_ref
  114.7 10.0 %all-to-all-done.3.m_ref = f32[4,7,64,128]{3,2,1,0:T(8,128)S(1)} async-done(((f32[4,7,64,128]{3,2,1,0:T(8,128)}), f32[4,7,64,128]{3,2,1,0:T(8,128)S(1)}, u32[]{:S(2)}, u32[]{:S(2)}) %all-to-all-start.3) | async-done | bytes 917536 | tf_op jit(solution)/shard_map/all_to_all | solution.py:323
  124.7 13.6 %final.1 = bf16[1,12,48,3072]{3,2,1,0:T(8,128)(2,1)} custom-call(f32[12,28]{1,0:T(8,128)S(1)} %copy.24.z_ref, f32[4,7,64,128]{3,2,1,0:T(8,128)S(1)} %all-to-all-done.3.m_ref, f32[12,48,3072]{2,1,0:T(8,128)} %get-tuple-element.10.slope_ref, bf16[256,256]{1,0:T(8,128)(2,1)S(1)} %mul.51.w_ref, bf16[48,48]{1,0:T(8,128)(2,1)S(1)} %copy-done.11, ...), custom_call_target="tpu_custom_call" | custom-call | tf_op jit(solution)/shard_map/final/pallas_call | solution.py:379
  138.4 0.0 all-gather.5.cloned.1.call-done
  138.4 18.2 %all-gather.7.cloned.1.call-done = f32[56,64,128]{2,1,0:T(8,128)} async-done(((f32[7,64,128]{2,1,0:T(8,128)}), f32[56,64,128]{2,1,0:T(8,128)}) %all-gather.7.cloned.1.call-update) | async-done | bytes 1835024 | tf_op jit(solution)/shard_map/all_gather | solution.py:342
  156.6 0.0 copy-start.2
  156.6 1.5 copy-done.2
  158.1 0.0 copy-start.3
  158.1 1.5 copy-done.3
  159.6 26.1 %grads.1 = f32[2,7,64,4096]{3,2,1,0:T(8,128)} custom-call(f32[3584,128]{1,0:T(8,128)S(1)} %bitcast.9, f32[3584,128]{1,0:T(8,128)S(1)} %bitcast.8), custom_call_target="tpu_custom_call" | custom-call | flops 2147483648 | bytes 67108864 | tf_op jit(solution)/shard_map/grads/pallas_call | solution.py:393
  (3 shorter events, 0.0 us)
Async XLA Ops:
  8.1 0.7 copy-start.6
  8.8 0.7 copy-start.8
  9.5 0.7 copy-start.12
  10.2 0.7 copy-start.15
  10.9 28.8 %copy-start.5 = (bf16[128,4096]{1,0:T(8,128)(2,1)S(1)}, bf16[128,4096]{1,0:T(8,128)(2,1)}, u32[]{:S(2)}) copy-start(bf16[128,4096]{1,0:T(8,128)(2,1)} %constant.40.clone.e_ref) | copy-start | bytes 3145732
  39.6 7.8 %copy-start = (f32[7,64,128]{2,1,0:T(8,128)}, f32[7,64,128]{2,1,0:T(8,128)S(1)}, u32[]{:S(2)}) copy-start(f32[7,64,128]{2,1,0:T(8,128)S(1)} %reduce_sum.18.spec_ref) | copy-start | bytes 688132
  39.7 11.4 %copy-start.17 = (f32[64]{0:T(128)S(1)}, f32[64]{0:T(128)}, u32[]{:S(2)}) copy-start(f32[64]{0:T(128)} %param.19) | copy-start | bytes 772
  39.7 11.5 %copy-start.16 = (bf16[64,64]{1,0:T(8,128)(2,1)S(1)}, bf16[64,64]{1,0:T(8,128)(2,1)}, u32[]{:S(2)}) copy-start(bf16[64,64]{1,0:T(8,128)(2,1)} %param.18) | copy-start | bytes 24580
  39.7 22.2 %copy-start.7 = (f32[16,128]{1,0:T(8,128)S(1)}, f32[16,128]{1,0:T(8,128)}, u32[]{:S(2)}) copy-start(f32[16,128]{1,0:T(8,128)} %constant.38.clone.tws_ref) | copy-start | bytes 24580
  39.7 22.2 %copy-start.9 = (f32[16,128]{1,0:T(8,128)S(1)}, f32[16,128]{1,0:T(8,128)}, u32[]{:S(2)}) copy-start(f32[16,128]{1,0:T(8,128)} %constant.37.clone.twc_ref) | copy-start | bytes 24580
  39.7 22.2 %copy-start.10 = (bf16[48,96]{1,0:T(8,128)(2,1)S(1)}, bf16[48,96]{1,0:T(8,128)(2,1)}, u32[]{:S(2)}) copy-start(bf16[48,96]{1,0:T(8,128)(2,1)} %constant.36.clone.ix_ref) | copy-start | bytes 27652
  39.7 22.2 %copy-start.11 = (bf16[48,48]{1,0:T(8,128)(2,1)S(1)}, bf16[48,48]{1,0:T(8,128)(2,1)}, u32[]{:S(2)}) copy-start(bf16[48,48]{1,0:T(8,128)(2,1)} %constant.35.clone.iy_ref) | copy-start | bytes 13828
  39.7 22.2 %copy-start.13 = (bf16[32,72]{1,0:T(8,128)(2,1)S(1)}, bf16[32,72]{1,0:T(8,128)(2,1)}, u32[]{:S(2)}) copy-start(bf16[32,72]{1,0:T(8,128)(2,1)} %constant.34.clone.fy_ref) | copy-start | bytes 13828
  39.8 22.2 %copy-start.14 = (bf16[32,144]{1,0:T(8,128)(2,1)S(1)}, bf16[32,144]{1,0:T(8,128)(2,1)}, u32[]{:S(2)}) copy-start(bf16[32,144]{1,0:T(8,128)(2,1)} %constant.33.clone.fx_ref) | copy-start | bytes 27652
  47.5 14.4 %all-to-all-start.1 = ((f32[4,7,64,128]{3,2,1,0:T(8,128)}), f32[4,7,64,128]{3,2,1,0:T(8,128)S(1)}, u32[]{:S(2)}, u32[]{:S(2)}) async-start(f32[4,7,64,128]{3,2,1,0:T(8,128)} %mix.1), calls=%async_computation.1 | async-start | bytes 1835008 | tf_op jit(solution)/shard_map/all_to_all | solution.py:323
  51.0 87.4 %all-gather.5.cloned.1.call-start = ((), (), s32[]{:S(2)}) async-start(), calls=%async_computation.4 | async-start | bytes 2064384 | tf_op jit(solution)/shard_map/all_gather | solution.py:369
  86.1 16.2 %copy-start.4 = (bf16[4096,128]{1,0:T(8,128)(2,1)S(1)}, bf16[4096,128]{1,0:T(8,128)(2,1)}, u32[]{:S(2)}) copy-start(bf16[4096,128]{1,0:T(8,128)(2,1)} %constant.41.clone.f_ref) | copy-start | bytes 3145732
  101.6 55.0 %all-gather.7.cloned.1.call-start = ((), (), s32[]{:S(2)}) async-start(), calls=%async_computation.5 | async-start | bytes 2064384 | tf_op jit(solution)/shard_map/all_gather | solution.py:342
  102.4 0.9 copy-start.1
  111.0 13.7 %all-to-all-start.3 = ((f32[4,7,64,128]{3,2,1,0:T(8,128)}), f32[4,7,64,128]{3,2,1,0:T(8,128)S(1)}, u32[]{:S(2)}, u32[]{:S(2)}) async-start(f32[4,7,64,128]{3,2,1,0:T(8,128)} %back.1), calls=%async_computation.3 | async-start | bytes 1835008 | tf_op jit(solution)/shard_map/all_to_all | solution.py:323
  156.6 1.5 copy-start.2
  158.1 1.5 copy-start.3
Sparse Core Ops, SparseCore 0:
  101.7 26.6 all-gather.4
  130.0 26.4 all-gather.6

commit v4 on v3

--- a/solution.py
+++ b/solution.py
@@ -270,18 +270,24 @@
     base = pl.program_id(0) * block
     for k in range(zmodes):
         slot = k % 2
-        for q in range(block):
-            at = pl.ds(base + (k * pairs + q), samples, stride=zmodes * pairs)
-            a = v_ref[at, :]
-            b = c_ref[at, :]
-            left = jnp.concatenate([a, roll_half(a)], axis=0)
-            right = jnp.concatenate([b, sign * roll_half(b)], axis=0)
-            l_hi, l_lo = split(left)
-            r_hi, r_lo = split(right)
-            lhs = jnp.concatenate([l_hi, l_lo, l_hi], axis=0).astype(BF16)[:, :chan]
-            rhs = jnp.concatenate([r_hi, r_hi, r_lo], axis=0).astype(BF16)
-            x_ref[slot, q * chan:(q + 1) * chan, :] = lax.dot_general(
-                lhs, rhs, (((0,), (0,)), ((), ())), preferred_element_type=F32)
+        for q in range(0, block, 2):
+            sides = []
+            for pair in (q, q + 1):
+                at = pl.ds(base + (k * pairs + pair), samples, stride=zmodes * pairs)
+                a = v_ref[at, :]
+                b = c_ref[at, :]
+                l_hi, l_lo = split(jnp.concatenate([a, roll_half(a)], axis=0))
+                r_hi, r_lo = split(jnp.concatenate([b, sign * roll_half(b)], axis=0))
+                sides.append((jnp.concatenate([l_hi, l_lo, l_hi], axis=0).astype(BF16),
+                              jnp.concatenate([r_hi, r_hi, r_lo], axis=0).astype(BF16)))
+            (l_one, r_one), (l_two, r_two) = sides
+            none = jnp.zeros_like(r_one)
+            lhs = jnp.concatenate([l_one, l_two], axis=0)[:, :chan]
+            rhs = jnp.concatenate([jnp.concatenate([r_one, none], axis=1),
+                                   jnp.concatenate([none, r_two], axis=1)], axis=0)
+            both = lax.dot_general(lhs, rhs, (((0,), (0,)), ((), ())), preferred_element_type=F32)
+            x_ref[slot, q * chan:(q + 1) * chan, :] = both[:, :LANES]
+            x_ref[slot, (q + 1) * chan:(q + 2) * chan, :] = both[:, LANES:]
         for j in range(chan // 2):
             even = x_ref[slot, pl.ds(2 * j, block, stride=chan), :]
             odd = x_ref[slot, pl.ds(2 * j + 1, block, stride=chan), :]
@@ -365,6 +371,7 @@
         compiler_params=params, name="middle",
     )(z_table, exchange(mixed), inputs, cotangent, w_wide, bias, iy, ix, fx3, fy, twc, tws)
 
+    all_spectra, cot_partial = lax.optimization_barrier((all_spectra, cot_partial))
     cot_spectrum = jnp.sum(exchange(cot_partial), axis=0)
     all_cots = lax.all_gather(cot_spectrum, "dp")
     back = pl.pallas_call(

time: 194 us -> 172 us (0.89)
  waiting for transfers between devices: 39.1 us -> 20.2 us
  Pallas kernels: 90.3 us -> 87.3 us
    all_gather x1, waiting for transfers between devices: 18.2 us -> 0.01 us  [on_device(): all_spectra = lax.all_gather(spectrum, 'dp')]
    pallas_call x1, Pallas kernels: 26.1 us -> 23 us  [on_device(): pl.pallas_call(functools.partial(grads_kernel, samples, pairs_here), grid...]
  transfers between devices with their start and end apart: 4 -> 4, of which waited for: 3 -> 2; matrix products, arithmetic and copies ran while one was open for 0% -> 1% of each run, Pallas kernels for 11% -> 31%
where the time goes in v4:
time: 172 us; the launch traced here: 171 us
  Pallas kernels  87.3 us (51%)
  blocking collectives  32.5 us (19%)
  waiting for transfers between devices  20.2 us (12%)
  between operations  14.2 us (8%)
  local copies, waits for them, and re-layouts  7.71 us (4%)
  starting transfers between devices  7.09 us (4%)
  other arithmetic  1.74 us (1%)
    all_to_all x2, blocking collectives, exchange(): return lax.all_to_all(x, 'mp', 0, 0)  32.5 us
    pallas_call x1, Pallas kernels, on_device(): pl.pallas_call(functools.partial(middle_kernel, zmodes, half), grid=(plan...  24.1 us
    pallas_call x1, Pallas kernels, on_device(): pl.pallas_call(functools.partial(grads_kernel, samples, pairs_here), grid...  23 us
    all_to_all x2, waiting for transfers between devices, exchange(): return lax.all_to_all(x, 'mp', 0, 0)  20.2 us
    pallas_call x1, Pallas kernels, on_device(): pl.pallas_call(functools.partial(final_kernel, zmodes, half), grid=(plane...  13.8 us
    pallas_call x1, Pallas kernels, on_device(): pl.pallas_call(functools.partial(forward_kernel, zmodes, half), grid=(pla...  11 us
    pallas_call x1, Pallas kernels, on_device(): pl.pallas_call(mix_kernel, grid=(pairs_here // block,), in_specs=[m_spec,...  7.7 us
    pallas_call x1, Pallas kernels, on_device(): pl.pallas_call(back_kernel, grid=(pairs_here // block,), in_specs=[m_spec...  7.69 us
  transfers between devices with their start and end apart: 4, of which 2 were waited for; matrix products, arithmetic and copies ran while one was open for 1% of the time, Pallas kernels for 31%

profile of v4, /device:TPU:0, one launch (start us, length us, event | category | flops | bytes accessed | tf_op | source)
XLA Modules:
  0.0 170.8 jit_solution(8542506608590679591)
XLA Ops:
  7.2 0.0 all-gather.5.cloned.1.call-start
  7.2 0.8 constant_dynamic-slice_fusion
  8.0 0.1 copy.24.z_ref
  8.1 0.0 copy-start.6
  8.1 0.7 copy-done.6
  8.8 0.0 copy-start.8
  8.8 0.7 copy-done.8
  9.5 0.0 copy-start.12
  9.5 0.7 copy-done.12
  10.2 0.0 copy-start.15
  10.2 0.7 copy-done.15
  10.9 0.0 copy-start.5
  10.9 11.0 %forward.1 = f32[4,7,64,128]{3,2,1,0:T(8,128)S(1)} custom-call(f32[12,28]{1,0:T(8,128)S(1)} %copy.24.z_ref, bf16[1,12,48,3072]{3,2,1,0:T(8,128)(2,1)} %x_ref.3, bf16[64,48]{1,0:T(8,128)(2,1)S(1)} %copy-done.15, bf16[32,72]{1,0:T(8,128)(2,1)S(1)} %copy-done.12, f32[16,128]{1,0:T(8,128)S(1)} %copy-done.8, f32[16,128]{1,0:T(8,128)S(1)} %copy-done.6), custom_call_target="tpu_custom_call" | custom-call | tf_op jit(solution)/shard_map/forward/pallas_call | solution.py:331
  21.9 17.7 %all_to_all.20 = f32[4,7,64,128]{3,2,1,0:T(8,128)S(1)} all-to-all(f32[4,7,64,128]{3,2,1,0:T(8,128)S(1)} %forward.1), channel_id=1, replica_groups=mesh['dp'=8,'mp'=4] {'mp'}, dimensions={0} | all-to-all | bytes 1835008 | tf_op jit(solution)/shard_map/all_to_all | solution.py:329
  39.6 0.7 reduce_sum.18.spec_ref
  40.4 0.0 all-gather.5.cloned.1.call-update
  40.4 0.0 copy-done.5
  40.4 0.0 copy-start
  40.4 0.9 copy-done
  41.3 0.0 copy-start.17
  41.4 0.0 copy-start.16
  41.4 0.0 copy-start.7
  41.4 0.0 copy-start.9
  41.4 0.0 copy-start.10
  41.4 0.0 copy-start.11
  41.4 0.0 copy-start.13
  41.4 0.0 copy-start.14
  41.4 7.7 %mix.1 = f32[4,7,64,128]{3,2,1,0:T(8,128)} custom-call(f32[7,64,128]{2,1,0:T(8,128)S(1)} %copy-done, bf16[2,7,64,4096]{3,2,1,0:T(8,128)(2,1)} %bitcast.11, bf16[128,4096]{1,0:T(8,128)(2,1)S(1)} %copy-done.5), custom_call_target="tpu_custom_call" | custom-call | tf_op jit(solution)/shard_map/mix/pallas_call | solution.py:349
  49.1 3.5 %all-to-all-start.1 = ((f32[4,7,64,128]{3,2,1,0:T(8,128)}), f32[4,7,64,128]{3,2,1,0:T(8,128)S(1)}, u32[]{:S(2)}, u32[]{:S(2)}) async-start(f32[4,7,64,128]{3,2,1,0:T(8,128)} %mix.1), calls=%async_computation.1 | async-start | bytes 1835008 | tf_op jit(solution)/shard_map/all_to_all | solution.py:329
  52.6 0.0 all-gather.7.cloned.1.call-start
  52.7 0.0 copy-done.17
  52.7 0.1 broadcast_in_dim_tile.3.b_ref
  52.8 0.0 copy-done.16
  52.8 0.1 copy.25
  52.9 0.3 broadcast_multiply_fusion
  53.2 0.2 mul.48.w_ref
  53.4 10.1 %all-to-all-done.1.m_ref = f32[4,7,64,128]{3,2,1,0:T(8,128)S(1)} async-done(((f32[4,7,64,128]{3,2,1,0:T(8,128)}), f32[4,7,64,128]{3,2,1,0:T(8,128)S(1)}, u32[]{:S(2)}, u32[]{:S(2)}) %all-to-all-start.1) | async-done | bytes 917536 | tf_op jit(solution)/shard_map/all_to_all | solution.py:329
  63.5 0.0 copy-done.7
  63.5 0.0 copy-done.9
  63.5 0.0 copy-done.10
  63.5 0.0 copy-done.11
  63.5 0.0 copy-done.13
  63.5 0.0 copy-done.14
  63.6 24.1 %middle.1 = (bf16[1,12,48,3072]{3,2,1,0:T(8,128)(2,1)}, f32[12,48,3072]{2,1,0:T(8,128)}, f32[4,7,64,128]{3,2,1,0:T(8,128)S(1)}) custom-call(f32[12,28]{1,0:T(8,128)S(1)} %copy.24.z_ref, f32[4,7,64,128]{3,2,1,0:T(8,128)S(1)} %all-to-all-done.1.m_ref, bf16[1,12,48,3072]{3,2,1,0:T(8,128)(2,1)} %x_ref.3, bf16[1,12,48,3072]{3,2,1,0:T(8,128)(2,1)} %ct_ref.1, ...), custom_call_target="tpu_custom_call" | custom-call | tf_op jit(solution)/shard_map/middle/pallas_call | solution.py:362
  87.7 0.0 copy-start.4
  87.7 0.0 all-gather.5.cloned.1.call-done
  87.7 14.8 %all_to_all.21 = f32[4,7,64,128]{3,2,1,0:T(8,128)S(1)} all-to-all(f32[4,7,64,128]{3,2,1,0:T(8,128)S(1)} %get-tuple-element.12), channel_id=1, replica_groups=mesh['dp'=8,'mp'=4] {'mp'}, dimensions={0} | all-to-all | bytes 1835008 | tf_op jit(solution)/shard_map/all_to_all | solution.py:329
  102.6 0.7 reduce_sum.19.spec_ref
  103.3 0.0 all-gather.7.cloned.1.call-update
  103.3 0.0 copy-done.4
  103.3 0.0 copy-start.1
  103.3 0.9 copy-done.1
  104.3 7.7 %back.1 = f32[4,7,64,128]{3,2,1,0:T(8,128)} custom-call(f32[7,64,128]{2,1,0:T(8,128)S(1)} %copy-done.1, bf16[2,7,64,4096]{3,2,1,0:T(8,128)(2,1)} %bitcast.12, bf16[4096,128]{1,0:T(8,128)(2,1)S(1)} %copy-done.4), custom_call_target="tpu_custom_call" | custom-call | tf_op jit(solution)/shard_map/back/pallas_call | solution.py:377
  111.9 3.5 %all-to-all-start.3 = ((f32[4,7,64,128]{3,2,1,0:T(8,128)}), f32[4,7,64,128]{3,2,1,0:T(8,128)S(1)}, u32[]{:S(2)}, u32[]{:S(2)}) async-start(f32[4,7,64,128]{3,2,1,0:T(8,128)} %back.1), calls=%async_computation.3 | async-start | bytes 1835008 | tf_op jit(solution)/shard_map/all_to_all | solution.py:329
  115.5 0.2 mul.51.w_ref
  115.7 10.0 %all-to-all-done.3.m_ref = f32[4,7,64,128]{3,2,1,0:T(8,128)S(1)} async-done(((f32[4,7,64,128]{3,2,1,0:T(8,128)}), f32[4,7,64,128]{3,2,1,0:T(8,128)S(1)}, u32[]{:S(2)}, u32[]{:S(2)}) %all-to-all-start.3) | async-done | bytes 917536 | tf_op jit(solution)/shard_map/all_to_all | solution.py:329
  125.7 0.0 copy-start.2
  125.7 13.8 %final.1 = bf16[1,12,48,3072]{3,2,1,0:T(8,128)(2,1)} custom-call(f32[12,28]{1,0:T(8,128)S(1)} %copy.24.z_ref, f32[4,7,64,128]{3,2,1,0:T(8,128)S(1)} %all-to-all-done.3.m_ref, f32[12,48,3072]{2,1,0:T(8,128)} %get-tuple-element.13.slope_ref, bf16[256,256]{1,0:T(8,128)(2,1)S(1)} %mul.51.w_ref, bf16[48,48]{1,0:T(8,128)(2,1)S(1)} %copy-done.11, ...), custom_call_target="tpu_custom_call" | custom-call | tf_op jit(solution)/shard_map/final/pallas_call | solution.py:386
  139.5 0.0 all-gather.7.cloned.1.call-done
  139.5 0.0 copy-done.2
  139.5 0.0 copy-start.3
  139.5 1.5 copy-done.3
  141.0 23.0 %grads.1 = f32[2,7,64,4096]{3,2,1,0:T(8,128)} custom-call(f32[3584,128]{1,0:T(8,128)S(1)} %bitcast.9, f32[3584,128]{1,0:T(8,128)S(1)} %bitcast.10), custom_call_target="tpu_custom_call" | custom-call | flops 2147483648 | bytes 67108864 | tf_op jit(solution)/shard_map/grads/pallas_call | solution.py:400
  (3 shorter events, 0.0 us)
Async XLA Ops:
  7.2 80.5 %all-gather.5.cloned.1.call-start = ((), (), s32[]{:S(2)}) async-start(), calls=%async_computation.4 | async-start | bytes 2064384 | tf_op jit(solution)/shard_map/all_gather | solution.py:348
  8.1 0.7 copy-start.6
  8.8 0.7 copy-start.8
  9.5 0.7 copy-start.12
  10.2 0.7 copy-start.15
  10.9 29.5 %copy-start.5 = (bf16[128,4096]{1,0:T(8,128)(2,1)S(1)}, bf16[128,4096]{1,0:T(8,128)(2,1)}, u32[]{:S(2)}) copy-start(bf16[128,4096]{1,0:T(8,128)(2,1)} %constant.40.clone.e_ref) | copy-start | bytes 3145732
  40.4 0.9 copy-start
  41.3 11.3 %copy-start.17 = (f32[64]{0:T(128)S(1)}, f32[64]{0:T(128)}, u32[]{:S(2)}) copy-start(f32[64]{0:T(128)} %param.19) | copy-start | bytes 772
  41.4 11.4 %copy-start.16 = (bf16[64,64]{1,0:T(8,128)(2,1)S(1)}, bf16[64,64]{1,0:T(8,128)(2,1)}, u32[]{:S(2)}) copy-start(bf16[64,64]{1,0:T(8,128)(2,1)} %param.18) | copy-start | bytes 24580
  41.4 22.2 %copy-start.7 = (f32[16,128]{1,0:T(8,128)S(1)}, f32[16,128]{1,0:T(8,128)}, u32[]{:S(2)}) copy-start(f32[16,128]{1,0:T(8,128)} %constant.38.clone.tws_ref) | copy-start | bytes 24580
  41.4 22.2 %copy-start.9 = (f32[16,128]{1,0:T(8,128)S(1)}, f32[16,128]{1,0:T(8,128)}, u32[]{:S(2)}) copy-start(f32[16,128]{1,0:T(8,128)} %constant.37.clone.twc_ref) | copy-start | bytes 24580
  41.4 22.2 %copy-start.10 = (bf16[48,96]{1,0:T(8,128)(2,1)S(1)}, bf16[48,96]{1,0:T(8,128)(2,1)}, u32[]{:S(2)}) copy-start(bf16[48,96]{1,0:T(8,128)(2,1)} %constant.36.clone.ix_ref) | copy-start | bytes 27652
  41.4 22.2 %copy-start.11 = (bf16[48,48]{1,0:T(8,128)(2,1)S(1)}, bf16[48,48]{1,0:T(8,128)(2,1)}, u32[]{:S(2)}) copy-start(bf16[48,48]{1,0:T(8,128)(2,1)} %constant.35.clone.iy_ref) | copy-start | bytes 13828
  41.4 22.2 %copy-start.13 = (bf16[32,72]{1,0:T(8,128)(2,1)S(1)}, bf16[32,72]{1,0:T(8,128)(2,1)}, u32[]{:S(2)}) copy-start(bf16[32,72]{1,0:T(8,128)(2,1)} %constant.34.clone.fy_ref) | copy-start | bytes 13828
  41.4 22.2 %copy-start.14 = (bf16[32,144]{1,0:T(8,128)(2,1)S(1)}, bf16[32,144]{1,0:T(8,128)(2,1)}, u32[]{:S(2)}) copy-start(bf16[32,144]{1,0:T(8,128)(2,1)} %constant.33.clone.fx_ref) | copy-start | bytes 27652
  49.1 14.4 %all-to-all-start.1 = ((f32[4,7,64,128]{3,2,1,0:T(8,128)}), f32[4,7,64,128]{3,2,1,0:T(8,128)S(1)}, u32[]{:S(2)}, u32[]{:S(2)}) async-start(f32[4,7,64,128]{3,2,1,0:T(8,128)} %mix.1), calls=%async_computation.1 | async-start | bytes 1835008 | tf_op jit(solution)/shard_map/all_to_all | solution.py:329
  52.6 86.8 %all-gather.7.cloned.1.call-start = ((), (), s32[]{:S(2)}) async-start(), calls=%async_computation.5 | async-start | bytes 2064384 | tf_op jit(solution)/shard_map/all_gather | solution.py:376
  87.7 15.6 %copy-start.4 = (bf16[4096,128]{1,0:T(8,128)(2,1)S(1)}, bf16[4096,128]{1,0:T(8,128)(2,1)}, u32[]{:S(2)}) copy-start(bf16[4096,128]{1,0:T(8,128)(2,1)} %constant.41.clone.f_ref) | copy-start | bytes 3145732
  103.3 0.9 copy-start.1
  111.9 13.8 %all-to-all-start.3 = ((f32[4,7,64,128]{3,2,1,0:T(8,128)}), f32[4,7,64,128]{3,2,1,0:T(8,128)S(1)}, u32[]{:S(2)}, u32[]{:S(2)}) async-start(f32[4,7,64,128]{3,2,1,0:T(8,128)} %back.1), calls=%async_computation.3 | async-start | bytes 1835008 | tf_op jit(solution)/shard_map/all_to_all | solution.py:329
  125.7 13.8 %copy-start.2 = (f32[56,64,128]{2,1,0:T(8,128)S(1)}, f32[56,64,128]{2,1,0:T(8,128)}, u32[]{:S(2)}) copy-start(f32[56,64,128]{2,1,0:T(8,128)} %all-gather.5.cloned.1.call-done) | copy-start | bytes 5505028
  139.5 1.5 copy-start.3
Sparse Core Ops, SparseCore 0:
  40.5 26.6 all-gather.4
  103.4 26.6 all-gather.6
